TPU v7x, 768 devices: a whole 4x8x12 slice. The times are simulated.
768 devices in a mesh: band: 32 (over y, z_lo), dom: 24 (over z_hi, x, core).
Axes of the slice: x: 4, y: 8, z: 12 (z_hi: 3, z_lo: 4; z = z_hi * 4 + z_lo), core: 2. Of those that a mesh axis runs over, the one named last changes fastest.
Arguments:
- states_in: float32 [256, 73728], P('band', 'dom'), may hold values from -6 to 6
- cell_nodes: int32 [384, 343], P('dom'), may hold values from 0 to 3839, as said below
- cell_scale: float32 [384], P('dom'), may hold values from 0.3 to 3
- cell_matrix: bfloat16 [343, 343], replicated
- node_scale: float32 [73728], P('dom'), may hold values from 0.5 to 2
- potential: float32 [73728], P('dom'), may hold values from -1 to 1
Outputs:
- filtered: bfloat16 [256, 73728], P('band', 'dom')
- gram: float32 [256, 256], P('band')
Inputs may be any that keep to these rules, and one draw needn't show every extreme that they name: `cell_nodes`: each cell's nodes lie within its own domain's owned nodes and the 384-node rims of the two neighbouring domains; the first cell of every domain touches its lower rim's first node and the last cell its upper rim's last node.
All inputs are finite; a program needn't handle non-finite values.
Results may differ from a plain program's by a relative error of at most 0.0075.
Values may be sent and summed in bfloat16 or wider, within the bound.
A program may use at most 32 MiB of HBM per device.

v0:
```python
import jax
import jax.numpy as jnp
from jax import lax
from jax.sharding import PartitionSpec as P

DEGREE = 3


filter_center = 0.25
filter_half = 1.5


def padded(value, sides, width):
    for axis, dim in sides:
        size, length = (lax.axis_size(axis), value.shape[dim])
        up = [(i, (i + 1) % size) for i in range(size - 1)]
        down = [(j, i) for i, j in up]
        last = lax.slice_in_dim(value, length - width, length, axis=dim)
        leading = lax.slice_in_dim(value, 0, width, axis=dim)
        before = lax.ppermute(last, axis, up)
        after = lax.ppermute(leading, axis, down)
        value = jnp.concatenate([before, value, after], axis=dim)
    return value


def local(states_in, cell_nodes, cell_scale, cell_matrix, node_scale, potential):
    group_size = states_in.shape[0]
    owned_len = states_in.shape[1]
    rim_width = owned_len // 8
    nodes_all = owned_len * lax.axis_size("dom")

    def apply_one(vector_in):
        weighted = (node_scale[None, :] * vector_in).astype(jnp.bfloat16)
        extended = padded(weighted, (("dom", 1),), rim_width)
        picked = extended[:, cell_nodes]
        cellwise = jnp.einsum(
            "ij,scj->sci", cell_matrix, picked, preferred_element_type=jnp.float32
        )
        cellwise = cellwise * cell_scale[None, :, None]
        assembled = jnp.zeros(extended.shape, jnp.float32).at[:, cell_nodes].add(cellwise)
        owned = assembled[:, rim_width : rim_width + owned_len]
        rim_sums = jnp.concatenate(
            [assembled[:, :rim_width], assembled[:, rim_width + owned_len :]], axis=1
        )
        returned = padded(rim_sums, (("dom", 1),), rim_width)
        middle = jnp.zeros((group_size, owned_len - 2 * rim_width), jnp.float32)
        owned = owned + jnp.concatenate(
            [returned[:, :rim_width], middle, returned[:, 3 * rim_width :]], axis=1
        )
        return node_scale[None, :] * owned + potential[None, :] * vector_in

    previous = states_in
    current = (apply_one(states_in) - filter_center * states_in) / filter_half
    for step in range(DEGREE - 1):
        following = 2.0 * (apply_one(current) - filter_center * current) / filter_half - previous
        previous = current
        current = following
    filtered = current.astype(jnp.bfloat16)
    columns = lax.all_to_all(filtered, "band", split_axis=1, concat_axis=0, tiled=True)
    partial_all = jnp.dot(columns, columns.T, preferred_element_type=jnp.float32)
    gram_whole = lax.psum(partial_all, ("band", "dom"))
    row_block = lax.dynamic_slice_in_dim(
        gram_whole, lax.axis_index("band") * group_size, group_size, 0
    )
    gram = row_block / nodes_all
    return (filtered, gram)


def solution(mesh):
    in_specs = (P("band", "dom"), P("dom", None), P("dom"), P(), P("dom"), P("dom"))
    out_specs = (P("band", "dom"), P("band", None))
    return jax.shard_map(local, mesh=mesh, in_specs=in_specs, out_specs=out_specs, check_vma=False)
```

profile of v0, /device:TPU:1, one launch (start us, length us, event | category | flops | bytes accessed | tf_op | source)
XLA Modules:
  0.0 736.8 jit_solution(10483522921378566518)
XLA Ops:
  7.2 0.9 multiply_convert_fusion.2
  8.2 4.5 collective-permute-start
  12.7 9.2 %collective-permute-start.1 = (bf16[8,384]{1,0:T(8,128)(2,1)S(1)}, bf16[8,384]{1,0:T(8,128)(2,1)S(1)}, u32[]{:S(2)}, u32[]{:S(2)}) collective-permute-start(bf16[8,384]{1,0:T(8,128)(2,1)S(1)} %get-tuple-element.21), channel_id=1, source_target_pairs={{1,0},{2,1},{3,2},{4,3},{5,4},{6,5},{7,6},{8,7},{9,8},{10,9},{11,1... | collective-permute-start | bytes 18440 | tf_op jit(solution)/shard_map/ppermute | solution.py:21
  21.9 0.7 compare_select_fusion
  22.7 0.1 reshape.52
  22.8 0.5 copy.129
  23.3 10.9 %gather_fusion = bf16[5488,8]{1,0:T(8,128)(2,1)S(1)} fusion(bf16[8,3840]{0,1:T(8,128)(2,1)S(1)} %copy.129, s32[6144]{0:T(1024)S(1)} %pad_clamp_fusion), kind=kCustom, calls=%fused_computation | custom fusion | bytes 197568 | tf_op jit(solution)/shard_map/gather | solution.py:35
  34.2 0.4 copy.130
  34.7 0.2 reshape.15
  34.9 0.2 fusion.2
  35.1 0.1 reshape.38
  35.3 2.4 copy.131
  37.6 31.4 %scatter_custom_fusion = f32[8,3840]{0,1:T(8,128)S(1)} fusion(s32[5488]{0:T(1024)S(1)} %reshape.52, f32[5488,8]{1,0:T(8,128)} %copy.131, f32[]{:T(128)} %constant.12.clone.1), kind=kCustom, calls=%fused_computation.16 | custom fusion | flops 43904 | bytes 123392 | tf_op jit(solution)/shard_map/scatter-add | solution.py:40
  69.0 1.9 collective-permute-start.2
  71.0 2.4 collective-permute-start.3
  73.5 1.3 slice.68
  74.7 1.8 copy.148
  76.6 0.1 copy.133
  76.7 1.3 collective-permute-done.3
  78.0 0.1 copy.134
  78.0 0.1 multiply_convert_fusion.1
  78.1 1.9 collective-permute-start.4
  80.1 2.4 collective-permute-start.5
  82.5 2.5 collective-permute-done.5
  85.0 0.5 copy.135
  85.5 10.9 %gather_fusion.1 = bf16[5488,8]{1,0:T(8,128)(2,1)S(1)} fusion(bf16[8,3840]{0,1:T(8,128)(2,1)S(1)} %copy.135, s32[6144]{0:T(1024)S(1)} %pad_clamp_fusion), kind=kCustom, calls=%fused_computation.1 | custom fusion | bytes 197568 | tf_op jit(solution)/shard_map/gather | solution.py:35
  96.4 0.4 copy.136
  96.9 0.2 reshape.23
  97.1 0.2 fusion.1
  97.3 0.1 reshape.46
  97.4 2.4 copy.137
  99.8 31.4 %scatter_custom_fusion.1 = f32[8,3840]{0,1:T(8,128)S(1)} fusion(s32[5488]{0:T(1024)S(1)} %reshape.52, f32[5488,8]{1,0:T(8,128)} %copy.137, f32[]{:T(128)} %constant.12.clone.1), kind=kCustom, calls=%fused_computation.14 | custom fusion | flops 43904 | bytes 123392 | tf_op jit(solution)/shard_map/scatter-add | solution.py:40
  131.2 1.9 collective-permute-start.6
  133.2 2.4 collective-permute-start.7
  135.6 1.3 slice.73
  136.8 1.8 copy.149
  138.7 0.1 copy.139
  138.8 8.9 %collective-permute-done.7 = f32[8,384]{0,1:T(8,128)S(1)} collective-permute-done((f32[8,384]{0,1:T(8,128)S(1)}, f32[8,384]{0,1:T(8,128)S(1)}, u32[]{:S(2)}, u32[]{:S(2)}) %collective-permute-start.7) | collective-permute-done | bytes 12320 | tf_op jit(solution)/shard_map/ppermute | solution.py:21
  147.7 0.1 copy.140
  147.8 0.1 multiply_convert_fusion
  147.9 1.9 collective-permute-start.8
  149.8 2.6 collective-permute-start.9
  152.4 12.8 %collective-permute-done.9 = bf16[8,384]{1,0:T(8,128)(2,1)S(1)} collective-permute-done((bf16[8,384]{1,0:T(8,128)(2,1)S(1)}, bf16[8,384]{1,0:T(8,128)(2,1)S(1)}, u32[]{:S(2)}, u32[]{:S(2)}) %collective-permute-start.9) | collective-permute-done | bytes 6176 | tf_op jit(solution)/shard_map/ppermute | solution.py:21
  165.3 0.5 copy.141
  165.7 10.9 %gather_fusion.2 = bf16[5488,8]{1,0:T(8,128)(2,1)S(1)} fusion(bf16[8,3840]{0,1:T(8,128)(2,1)S(1)} %copy.141, s32[6144]{0:T(1024)S(1)} %pad_clamp_fusion), kind=kCustom, calls=%fused_computation.2 | custom fusion | bytes 197568 | tf_op jit(solution)/shard_map/gather | solution.py:35
  176.7 0.4 copy.142
  177.1 0.2 reshape.31
  177.3 0.2 fusion
  177.6 0.1 reshape.54
  177.7 2.4 copy.143
  180.1 31.4 %scatter_custom_fusion.2 = f32[8,3840]{0,1:T(8,128)S(1)} fusion(s32[5488]{0:T(1024)S(1)} %reshape.52, f32[5488,8]{1,0:T(8,128)} %copy.143, f32[]{:T(128)} %constant.12.clone.1), kind=kCustom, calls=%fused_computation.12 | custom fusion | flops 43904 | bytes 123392 | tf_op jit(solution)/shard_map/scatter-add | solution.py:40
  211.5 1.9 collective-permute-start.10
  213.4 2.4 collective-permute-start.11
  215.8 1.3 slice.78
  217.1 1.8 copy.150
  218.9 0.1 copy.145
  219.0 7.4 %collective-permute-done.11 = f32[8,384]{0,1:T(8,128)S(1)} collective-permute-done((f32[8,384]{0,1:T(8,128)S(1)}, f32[8,384]{0,1:T(8,128)S(1)}, u32[]{:S(2)}, u32[]{:S(2)}) %collective-permute-start.11) | collective-permute-done | bytes 12320 | tf_op jit(solution)/shard_map/ppermute | solution.py:21
  226.4 0.1 copy.146
  226.5 0.1 fusion.25
  226.6 0.1 all_to_all.14
  226.8 20.1 %all_to_all.19 = bf16[8,32,96]{2,0,1:T(8,128)(2,1)S(1)} all-to-all(bf16[8,32,96]{2,0,1:T(8,128)(2,1)S(1)} %copy.147), channel_id=1, replica_groups=mesh['band'=32,'dom'=24] {'band'}, dimensions={1} | all-to-all | bytes 98304 | tf_op jit(solution)/shard_map/all_to_all | solution.py:59
  246.9 0.9 fusion.29
  247.8 480.8 %all-reduce.2.cloned.1.call-done = f32[256,256]{1,0:T(8,128)} async-done(((f32[256,256]{1,0:T(8,128)}), f32[256,256]{1,0:T(8,128)}) %all-reduce.2.cloned.1.call-update) | async-done | bytes 262160 | tf_op jit(solution)/shard_map/psum | solution.py:61
  728.6 1.3 dynamic-slice_multiply_fusion
  (36 shorter events, 0.3 us)
Async XLA Ops:
  7.2 27.7 %copy-start = (bf16[343,343]{1,0:T(8,128)(2,1)S(1)}, bf16[343,343]{1,0:T(8,128)(2,1)}, u32[]{:S(2)}) copy-start(bf16[343,343]{1,0:T(8,128)(2,1)} %param.9) | copy-start | bytes 705898
  7.2 721.5 %all-reduce.2.cloned.1.call-start = ((), (), s32[]{:S(2)}) async-start(), calls=%async_computation.1 | async-start | bytes 524288 | tf_op jit(solution)/shard_map/psum | solution.py:61
  8.2 26.7 %copy-start.5 = (f32[16]{0:T(128)S(1)}, f32[16]{0:T(128)}, u32[]{:S(2)}) copy-start(f32[16]{0:T(128)} %param.8) | copy-start | bytes 196
  8.2 14.6 %collective-permute-start = (bf16[8,384]{1,0:T(8,128)(2,1)S(1)}, bf16[8,384]{1,0:T(8,128)(2,1)S(1)}, u32[]{:S(2)}, u32[]{:S(2)}) collective-permute-start(bf16[8,384]{1,0:T(8,128)(2,1)S(1)} %get-tuple-element.20), channel_id=1, source_target_pairs={{0,1},{1,2},{2,3},{3,4},{4,5},{5,6},{6,7},{7,8},{8,9},{9,10},{10,1... | collective-permute-start | bytes 18440 | tf_op jit(solution)/shard_map/ppermute | solution.py:20
  12.7 10.1 %collective-permute-start.1 = (bf16[8,384]{1,0:T(8,128)(2,1)S(1)}, bf16[8,384]{1,0:T(8,128)(2,1)S(1)}, u32[]{:S(2)}, u32[]{:S(2)}) collective-permute-start(bf16[8,384]{1,0:T(8,128)(2,1)S(1)} %get-tuple-element.21), channel_id=1, source_target_pairs={{1,0},{2,1},{3,2},{4,3},{5,4},{6,5},{7,6},{8,7},{9,8},{10,9},{11,1... | collective-permute-start | bytes 18440 | tf_op jit(solution)/shard_map/ppermute | solution.py:21
  37.6 35.8 %copy-start.2 = (f32[3072]{0:T(1024)S(1)}, f32[3072]{0:T(1024)}, u32[]{:S(2)}) copy-start(f32[3072]{0:T(1024)} %param.10) | copy-start | bytes 36868
  69.0 7.5 %collective-permute-start.2 = (f32[8,384]{0,1:T(8,128)S(1)}, f32[8,384]{0,1:T(8,128)S(1)}, u32[]{:S(2)}, u32[]{:S(2)}) collective-permute-start(f32[8,384]{0,1:T(8,128)S(1)} %get-tuple-element.14), channel_id=1, source_target_pairs={{0,1},{1,2},{2,3},{3,4},{4,5},{5,6},{6,7},{7,8},{8,9},{9,10},{10,1... | collective-permute-start | bytes 36872 | tf_op jit(solution)/shard_map/ppermute | solution.py:20
  71.0 7.0 collective-permute-start.3
  73.4 4.6 copy-start.1
  73.5 4.6 copy-start.3
  78.1 4.3 collective-permute-start.4
  80.1 4.9 collective-permute-start.5
  131.2 7.5 %collective-permute-start.6 = (f32[8,384]{0,1:T(8,128)S(1)}, f32[8,384]{0,1:T(8,128)S(1)}, u32[]{:S(2)}, u32[]{:S(2)}) collective-permute-start(f32[8,384]{0,1:T(8,128)S(1)} %get-tuple-element.12), channel_id=1, source_target_pairs={{0,1},{1,2},{2,3},{3,4},{4,5},{5,6},{6,7},{7,8},{8,9},{9,10},{10,1... | collective-permute-start | bytes 36872 | tf_op jit(solution)/shard_map/ppermute | solution.py:20
  133.2 14.5 %collective-permute-start.7 = (f32[8,384]{0,1:T(8,128)S(1)}, f32[8,384]{0,1:T(8,128)S(1)}, u32[]{:S(2)}, u32[]{:S(2)}) collective-permute-start(f32[8,384]{0,1:T(8,128)S(1)} %get-tuple-element.13), channel_id=1, source_target_pairs={{1,0},{2,1},{3,2},{4,3},{5,4},{6,5},{7,6},{8,7},{9,8},{10,9},{11,1... | collective-permute-start | bytes 36872 | tf_op jit(solution)/shard_map/ppermute | solution.py:21
  147.9 4.5 collective-permute-start.8
  149.8 15.4 %collective-permute-start.9 = (bf16[8,384]{1,0:T(8,128)(2,1)S(1)}, bf16[8,384]{1,0:T(8,128)(2,1)S(1)}, u32[]{:S(2)}, u32[]{:S(2)}) collective-permute-start(bf16[8,384]{1,0:T(8,128)(2,1)S(1)} %get-tuple-element.17), channel_id=1, source_target_pairs={{1,0},{2,1},{3,2},{4,3},{5,4},{6,5},{7,6},{8,7},{9,8},{10,9},{11,1... | collective-permute-start | bytes 18440 | tf_op jit(solution)/shard_map/ppermute | solution.py:21
  211.5 7.5 %collective-permute-start.10 = (f32[8,384]{0,1:T(8,128)S(1)}, f32[8,384]{0,1:T(8,128)S(1)}, u32[]{:S(2)}, u32[]{:S(2)}) collective-permute-start(f32[8,384]{0,1:T(8,128)S(1)} %get-tuple-element.10), channel_id=1, source_target_pairs={{0,1},{1,2},{2,3},{3,4},{4,5},{5,6},{6,7},{7,8},{8,9},{9,10},{10,1... | collective-permute-start | bytes 36872 | tf_op jit(solution)/shard_map/ppermute | solution.py:20
  213.4 13.0 %collective-permute-start.11 = (f32[8,384]{0,1:T(8,128)S(1)}, f32[8,384]{0,1:T(8,128)S(1)}, u32[]{:S(2)}, u32[]{:S(2)}) collective-permute-start(f32[8,384]{0,1:T(8,128)S(1)} %get-tuple-element.11), channel_id=1, source_target_pairs={{1,0},{2,1},{3,2},{4,3},{5,4},{6,5},{7,6},{8,7},{9,8},{10,9},{11,1... | collective-permute-start | bytes 36872 | tf_op jit(solution)/shard_map/ppermute | solution.py:21
  226.6 503.3 %copy-start.4 = (bf16[8,3072]{1,0:T(8,128)(2,1)}, bf16[8,3072]{1,0:T(8,128)(2,1)S(1)}, u32[]{:S(2)}) copy-start(bf16[8,3072]{1,0:T(8,128)(2,1)S(1)} %fusion.25) | copy-start | bytes 147460
Sparse Core Ops, SparseCore 0:
  247.9 480.6 all-reduce.1
where the time goes:
time: 737 us
  waiting for transfers between devices  514 us (70%)
  other arithmetic  97.4 us (13%)
  local copies, waits for them, and re-layouts  53.8 us (7%)
  starting transfers between devices  35.6 us (5%)
  blocking collectives  20.1 us (3%)
  between operations  14.5 us (2%)
    psum x1, waiting for transfers between devices, local(): gram_whole = lax.psum(partial_all, ('band', 'dom'))  481 us
    scatter-add x3, other arithmetic, apply_one(): jnp.zeros(extended.shape, jnp.float32).at[:, cell_nodes].add(cellwise)  94.1 us
    gather x9, local copies, waits for them, and re-layouts, apply_one(): picked = extended[:, cell_nodes]  34.7 us
    ppermute x6, waiting for transfers between devices, padded(): after = lax.ppermute(leading, axis, down)  33 us
    ppermute x6, starting transfers between devices, padded(): after = lax.ppermute(leading, axis, down)  21.4 us
    all_to_all x1, blocking collectives, local(): lax.all_to_all(filtered, 'band', split_axis=1, concat_axis=0, tiled=True)  20.1 us
  transfers between devices with their start and end apart: 13, of which 6 were waited for; matrix products, arithmetic and copies ran while one was open for 1% of the time, Pallas kernels for 0%

commit v1 on v0

v1 whole, which is shorter than its diff:
```python
import functools

import jax
import jax.numpy as jnp
from jax import lax
from jax.experimental import pallas as pl
from jax.experimental.pallas import tpu as pltpu
from jax.sharding import PartitionSpec as P

CENTER = 0.25
HALF = 1.5
MESH = pl.DeviceIdType.MESH
F32 = jnp.float32
BF16 = jnp.bfloat16

RIM_HI = (0, 1, 2, 3, 12, 13, 14, 15)
MID_HI = (4, 5, 6, 7, 8, 9, 10, 11)
LOW_TILES = ((0, 1), (1, 0), (1, 1), (2, 0), (2, 1), (3, 0))
UP_TILES = ((12, 1), (13, 0), (13, 1), (14, 0), (14, 1), (15, 0))
OWN_TILES = tuple((2 + t // 2, t % 2) for t in range(24))


def tile(ref, hi, half):
    return ref[8 * hi : 8 * hi + 8, 128 * half : 128 * half + 128]


def put(ref, hi, half, value):
    ref[8 * hi : 8 * hi + 8, 128 * half : 128 * half + 128] = value


def dot_t(a, b):
    return lax.dot_general(a, b, (((1,), (1,)), ((), ())), preferred_element_type=F32)


class Layout:
    def __init__(self, n_band, n_dom):
        self.n_band, self.n_dom = n_band, n_dom
        self.nz = 4 if n_band == 32 else 2
        self.ny = n_band // self.nz
        self.nx = 8 if n_dom == 24 else 2
        self.nh = n_dom // self.nx
        self.per = 24 // self.ny


def kernel(
    lay, nodes_all,
    states, nodes, cell_scale, matrix, node_scale, potential,
    filtered, gram,
    lt, le, mat, pad_nodes, hb, y0, y1, y2, ns, pc, acc, w2, mid, picked, x16, vh,
    stage, init_in, out_low, out_up, in_low, in_up, shares, got, part, part_in, sum1, sum1_in, sum2, sum2_in,
    send_sem, recv_sem, gram_send, gram_recv,
):
    band, dom = lax.axis_index("band"), lax.axis_index("dom")
    n_band, n_dom = lay.n_band, lay.n_dom
    left, right = lax.rem(dom + n_dom - 1, n_dom), lax.rem(dom + 1, n_dom)
    my_y, my_z = band // lay.nz, lax.rem(band, lay.nz)
    my_h, my_x = dom // lay.nx, lax.rem(dom, lay.nx)
    has_left, has_right = dom > 0, dom < n_dom - 1

    band_peers = [lax.rem(band + i, n_band) for i in range(1, n_band)]
    x_peers = [my_h * lay.nx + lax.rem(my_x + i, lay.nx) for i in range(1, lay.nx)]
    h_peers = [lax.rem(my_h + i, lay.nh) * lay.nx + my_x for i in range(1, lay.nh)]

    barrier = pltpu.get_barrier_semaphore()
    dom_peers = [left, right] + x_peers + h_peers
    for peer in dom_peers:
        pl.semaphore_signal(barrier, inc=1, device_id=(band, peer), device_id_type=MESH)
    for peer in band_peers:
        pl.semaphore_signal(barrier, inc=1, device_id=(peer, dom), device_id_type=MESH)

    pad_nodes[...] = jnp.full(pad_nodes.shape, -4096, jnp.int32)
    pad_nodes[:16, :343] = nodes[...]
    mat[...] = jnp.zeros(mat.shape, BF16)
    mat[:343, :343] = matrix[...]
    shifted = pad_nodes[...] + 128
    lo_all = shifted & 255
    hi_all = shifted >> 8
    lo_t = lo_all.T
    row_iota = lax.broadcasted_iota(jnp.int32, (256, 768), 0)
    lane_iota = lax.broadcasted_iota(jnp.int32, (384, 256), 1)
    for p in range(8):
        cols = slice(768 * p, 768 * p + 768)
        lo = jnp.concatenate([lo_all[2 * p : 2 * p + 1], lo_all[2 * p + 1 : 2 * p + 2]], axis=1)
        hi = jnp.concatenate([hi_all[2 * p : 2 * p + 1], hi_all[2 * p + 1 : 2 * p + 2]], axis=1)
        hb[p] = jnp.broadcast_to(hi, (8, 768))
        lt[:, cols] = jnp.where(row_iota == lo, 1.0, 0.0).astype(BF16)
        for c in (2 * p, 2 * p + 1):
            le[384 * c : 384 * c + 384, :] = jnp.where(
                lane_iota == lo_t[:, c : c + 1], 1.0, 0.0
            ).astype(BF16)

    for ref in (y0, ns, pc):
        ref[0:16] = jnp.zeros((16, 256), F32)
        ref[112:128] = jnp.zeros((16, 256), F32)
    for b in range(12):
        rows, cols = slice(16 + 8 * b, 24 + 8 * b), slice(256 * b, 256 * b + 256)
        y0[rows] = states[:, cols]
        ns[rows] = jnp.broadcast_to(node_scale[:, cols], (8, 256))
        pc[rows] = jnp.broadcast_to(potential[:, cols] - CENTER, (8, 256))
    for side, cols in ((0, slice(0, 384)), (1, slice(2688, 3072))):
        stage[side, 0:8] = states[:, cols]
        stage[side, 8:16] = jnp.concatenate(
            [node_scale[:, cols], potential[:, cols], jnp.zeros((6, 384), F32)], axis=0
        )

    pl.semaphore_wait(barrier, len(dom_peers) + len(band_peers))

    def rim_copy(src, dst, slot, to):
        copy = pltpu.make_async_remote_copy(
            src_ref=src, dst_ref=dst, send_sem=send_sem.at[slot], recv_sem=recv_sem.at[slot],
            device_id=(band, to), device_id_type=MESH,
        )
        copy.start()
        return copy

    started = [
        rim_copy(stage.at[0], init_in.at[1], 0, left),
        rim_copy(stage.at[1], init_in.at[0], 1, right),
    ]

    def gather(his, first):
        runs = [(his[0], his[-1] + 1)] if his == MID_HI else [(0, 4), (12, 16)]
        left_side = jnp.concatenate([w2[8 * a : 8 * b, :] for a, b in runs], axis=0)
        for p in range(8):
            cols = slice(768 * p, 768 * p + 768)
            t = jnp.dot(left_side, lt[:, cols], preferred_element_type=F32)
            index = hb[p]
            total = jnp.zeros((8, 768), F32) if first else mid[:, cols]
            for k, hi in enumerate(his):
                total = jnp.where(index == hi, t[8 * k : 8 * k + 8], total)
            if first:
                mid[:, cols] = total
            else:
                picked[16 * p : 16 * p + 16, :] = jnp.concatenate(
                    [total[:, :384], total[:, 384:]], axis=0
                ).astype(BF16)

    def scatter(his):
        for p in range(8):
            cols = slice(768 * p, 768 * p + 768)
            index = jnp.concatenate([hb[p], hb[p]], axis=0)
            x = x16[:, cols]
            for k, hi in enumerate(his):
                vh[16 * k : 16 * k + 16, cols] = jnp.where(index == hi, x, 0.0).astype(BF16)
        r = jnp.dot(vh[...], le[...], preferred_element_type=F32)
        for k, hi in enumerate(his):
            acc[8 * hi : 8 * hi + 8, :] = r[16 * k : 16 * k + 8] + r[16 * k + 8 : 16 * k + 16]

    def weigh(y, rows):
        w2[rows, :] = (ns[rows, :] * y[rows, :]).astype(BF16)

    def advance(step, rows, cols):
        now = (y0, y1, y2)[step][rows, cols]
        h = ns[rows, cols] * acc[rows, cols] + pc[rows, cols] * now
        if step == 0:
            y1[rows, cols] = h * (1.0 / HALF)
        elif step == 1:
            y2[rows, cols] = h * (2.0 / HALF) - y0[rows, cols]
        else:
            y1[rows, cols] = h * (2.0 / HALF) - y1[rows, cols]

    whole = slice(0, 256)
    middle, lower, upper = slice(32, 96), slice(0, 32), slice(96, 128)

    weigh(y0, middle)
    gather(MID_HI, True)
    for copy in started:
        copy.wait_recv()
    for side, tiles in ((0, LOW_TILES[:3]), (1, UP_TILES[3:])):
        there = has_left if side == 0 else has_right
        value = jnp.where(there, init_in[side], 0.0)
        for i, (hi, half) in enumerate(tiles):
            cols = slice(128 * i, 128 * i + 128)
            put(y0, hi, half, value[0:8, cols])
            put(ns, hi, half, jnp.broadcast_to(value[8:9, cols], (8, 128)))
            put(pc, hi, half, jnp.broadcast_to(value[9:10, cols] - CENTER, (8, 128)))
    weigh(y0, lower)
    weigh(y0, upper)
    gather(RIM_HI, False)

    gram_copies = []

    def send_share(share):
        for z in range(lay.nz):
            def go(share=share, z=z):
                pltpu.make_async_remote_copy(
                    src_ref=shares.at[share], dst_ref=got.at[band],
                    send_sem=gram_send.at[0], recv_sem=gram_recv.at[0],
                    device_id=(share * lay.nz + z, dom), device_id_type=MESH,
                ).start()
            pl.when(band != share * lay.nz + z)(go)

    def fill_shares(which):
        for share in which:
            tiles = OWN_TILES[lay.per * share : lay.per * share + lay.per]
            shares[share] = jnp.concatenate([tile(y1, *t) for t in tiles], axis=1).astype(BF16)
            filtered[:, 128 * lay.per * share : 128 * lay.per * (share + 1)] = shares[share]
            send_share(share)

    for step in range(3):
        cells = dot_t(picked[...], mat[...])
        for p in range(8):
            x = jnp.concatenate(
                [cells[16 * p : 16 * p + 8] * cell_scale[2 * p],
                 cells[16 * p + 8 : 16 * p + 16] * cell_scale[2 * p + 1]], axis=1)
            rest = x - x.astype(BF16).astype(F32)
            x16[:, 768 * p : 768 * p + 768] = jnp.concatenate([x, rest], axis=0)
        scatter(RIM_HI)
        last = step == 2
        low_tiles, up_tiles = (LOW_TILES[:3], UP_TILES[3:]) if last else (LOW_TILES, UP_TILES)
        for i, (lt_, ut_) in enumerate(zip(low_tiles, up_tiles)):
            out_low[step, 8 * i : 8 * i + 8] = tile(acc, *lt_)
            out_up[step, 8 * i : 8 * i + 8] = tile(acc, *ut_)
        rows = 8 * len(low_tiles)
        now = [
            rim_copy(out_low.at[step, 0:rows], in_up.at[step, 0:rows], 2 + 2 * step, left),
            rim_copy(out_up.at[step, 0:rows], in_low.at[step, 0:rows], 3 + 2 * step, right),
        ]
        started += now
        scatter(MID_HI)
        advance(step, middle, whole)
        if last:
            advance(step, slice(24, 32), slice(128, 256))
            advance(step, slice(96, 104), slice(0, 128))
            fill_shares(range(1, lay.ny - 1))
        else:
            weigh((y1, y2)[step], middle)
            gather(MID_HI, True)
        for copy in now:
            copy.wait_recv()
        low_to, up_to = (LOW_TILES[3:], UP_TILES[:3]) if last else (LOW_TILES, UP_TILES)
        for i, (lt_, ut_) in enumerate(zip(low_to, up_to)):
            got_low = jnp.where(has_left, in_low[step, 8 * i : 8 * i + 8], 0.0)
            got_up = jnp.where(has_right, in_up[step, 8 * i : 8 * i + 8], 0.0)
            put(acc, *lt_, tile(acc, *lt_) + got_low)
            put(acc, *ut_, tile(acc, *ut_) + got_up)
        if last:
            advance(step, slice(16, 24), whole)
            advance(step, slice(24, 32), slice(0, 128))
            advance(step, slice(96, 104), slice(128, 256))
            advance(step, slice(104, 112), whole)
            fill_shares((0, lay.ny - 1))
        else:
            advance(step, lower, whole)
            advance(step, upper, whole)
            weigh((y1, y2)[step], lower)
            weigh((y1, y2)[step], upper)
            gather(RIM_HI, False)

    def wait_bytes(ref, send, slot):
        sem = (gram_send if send else gram_recv).at[slot]
        pltpu.make_async_copy(ref, ref, sem).wait()

    got[band] = shares[my_y]
    wait_bytes(got.at[0 : n_band - 1], False, 0)
    columns = got[...].astype(F32).reshape(8 * n_band, 128 * lay.per).astype(BF16)
    rows = jnp.concatenate(
        [got[y * lay.nz + my_z].astype(F32) for y in range(lay.ny)], axis=0
    ).astype(BF16)
    part[...] = dot_t(rows, columns).reshape(lay.ny, 8, 8 * n_band)

    def reduce(peers, src, dst, slot, index, own):
        for device, piece in peers:
            pltpu.make_async_remote_copy(
                src_ref=src(piece), dst_ref=dst.at[index],
                send_sem=gram_send.at[slot], recv_sem=gram_recv.at[slot],
                device_id=device, device_id_type=MESH,
            ).start()
        dst[index] = own
        wait_bytes(dst.at[0 : len(peers)], False, slot)
        total = dst[0]
        for i in range(1, len(peers) + 1):
            total = total + dst[i]
        return total

    y_peers = [lax.rem(my_y + i, lay.ny) for i in range(1, lay.ny)]
    sum1[...] = reduce(
        [((y * lay.nz + my_z, dom), y) for y in y_peers],
        lambda piece: part.at[piece], part_in, 1, my_y, part[my_y],
    )
    sum2[...] = reduce(
        [((band, peer), None) for peer in x_peers], lambda piece: sum1, sum1_in, 2, my_x, sum1[...]
    )
    total = reduce(
        [((band, peer), None) for peer in h_peers], lambda piece: sum2, sum2_in, 3, my_h, sum2[...]
    )
    gram[...] = total * (1.0 / nodes_all)

    for copy in started:
        copy.wait_send()
    wait_bytes(got.at[0 : n_band - 1], True, 0)
    wait_bytes(part_in.at[0 : lay.ny - 1], True, 1)
    wait_bytes(sum1_in.at[0 : lay.nx - 1], True, 2)
    wait_bytes(sum2_in.at[0 : lay.nh - 1], True, 3)


def local(lay, states_in, cell_nodes, cell_scale, cell_matrix, node_scale, potential):
    owned = states_in.shape[1]
    cells = cell_nodes.shape[0] * 384
    vmem, smem = pl.BlockSpec(memory_space=pltpu.VMEM), pl.BlockSpec(memory_space=pltpu.SMEM)
    n_band, share = lay.n_band, 128 * lay.per
    return pl.pallas_call(
        functools.partial(kernel, lay, owned * lay.n_dom),
        out_shape=(
            jax.ShapeDtypeStruct((8, owned), BF16),
            jax.ShapeDtypeStruct((8, 8 * n_band), F32),
        ),
        in_specs=[vmem, vmem, smem, vmem, vmem, vmem],
        out_specs=(vmem, vmem),
        scratch_shapes=[
            pltpu.VMEM((256, cells), BF16),
            pltpu.VMEM((cells, 256), BF16),
            pltpu.VMEM((384, 384), BF16),
            pltpu.VMEM((128, 384), jnp.int32),
            pltpu.VMEM((8, 8, 768), jnp.int32),
            pltpu.VMEM((128, 256), F32),
            pltpu.VMEM((128, 256), F32),
            pltpu.VMEM((128, 256), F32),
            pltpu.VMEM((128, 256), F32),
            pltpu.VMEM((128, 256), F32),
            pltpu.VMEM((128, 256), F32),
            pltpu.VMEM((128, 256), BF16),
            pltpu.VMEM((8, cells), F32),
            pltpu.VMEM((128, 384), BF16),
            pltpu.VMEM((16, cells), F32),
            pltpu.VMEM((128, cells), BF16),
            pltpu.VMEM((2, 16, 384), F32),
            pltpu.VMEM((2, 16, 384), F32),
            pltpu.VMEM((3, 48, 128), F32),
            pltpu.VMEM((3, 48, 128), F32),
            pltpu.VMEM((3, 48, 128), F32),
            pltpu.VMEM((3, 48, 128), F32),
            pltpu.VMEM((lay.ny, 8, share), BF16),
            pltpu.VMEM((n_band, 8, share), BF16),
            pltpu.VMEM((lay.ny, 8, 8 * n_band), F32),
            pltpu.VMEM((lay.ny, 8, 8 * n_band), F32),
            pltpu.VMEM((8, 8 * n_band), F32),
            pltpu.VMEM((lay.nx, 8, 8 * n_band), F32),
            pltpu.VMEM((8, 8 * n_band), F32),
            pltpu.VMEM((lay.nh, 8, 8 * n_band), F32),
            pltpu.SemaphoreType.DMA((8,)),
            pltpu.SemaphoreType.DMA((8,)),
            pltpu.SemaphoreType.DMA((4,)),
            pltpu.SemaphoreType.DMA((4,)),
        ],
        compiler_params=pltpu.CompilerParams(
            collective_id=0, has_side_effects=True, vmem_limit_bytes=48 * 1024 * 1024
        ),
    )(states_in, cell_nodes, cell_scale, cell_matrix, node_scale[None, :], potential[None, :])


def solution(mesh):
    lay = Layout(mesh.shape["band"], mesh.shape["dom"])
    in_specs = (P("band", "dom"), P("dom", None), P("dom"), P(), P("dom"), P("dom"))
    out_specs = (P("band", "dom"), P("band", None))
    return jax.shard_map(
        functools.partial(local, lay), mesh=mesh, in_specs=in_specs, out_specs=out_specs, check_vma=False
    )
```

time: 737 us -> 69.7 us (0.09)
  waiting for transfers between devices: 514 us -> 0 us
  other arithmetic: 97.4 us -> 0 us
  Pallas kernels: 0 us -> 62 us
  local copies, waits for them, and re-layouts: 53.8 us -> 5.86 us
  starting transfers between devices: 35.6 us -> 0 us
  blocking collectives: 20.1 us -> 0 us
  between operations: 14.5 us -> 0.65 us
    psum x1 -> x0, waiting for transfers between devices: 481 us -> none  [local(): gram_whole = lax.psum(partial_all, ('band', 'dom'))]
    scatter-add x3 -> x0, other arithmetic: 94.1 us -> none  [apply_one(): jnp.zeros(extended.shape, jnp.float32).at[:, cell_nodes].add(cellwise)]
    pallas_call x0 -> x1, Pallas kernels: none -> 62 us  [local(): pl.pallas_call(functools.partial(kernel, lay, owned * lay.n_dom), out_sha...]
    ppermute x12 -> x0, starting transfers between devices: 35.5 us -> none  [the longest x6 21.4 us: padded(): after = lax.ppermute(leading, axis, down)]
    gather x9 -> x0, local copies, waits for them, and re-layouts: 34.7 us -> none  [apply_one(): picked = extended[:, cell_nodes]]
    ppermute x12 -> x0, waiting for transfers between devices: 33 us -> none  [the longest x6 33 us: padded(): after = lax.ppermute(leading, axis, down)]
    all_to_all x1 -> x0, blocking collectives: 20.1 us -> none  [local(): lax.all_to_all(filtered, 'band', split_axis=1, concat_axis=0, tiled=True)]
    mul x6 -> x0, local copies, waits for them, and re-layouts: 7.49 us -> none  [apply_one(): cellwise = cellwise * cell_scale[None, :, None]]
  transfers between devices with their start and end apart: 13 -> 0, of which waited for: 6 -> 0; matrix products, arithmetic and copies ran while one was open for 1% -> 0% of each run, Pallas kernels for 0% -> 0%
where the time goes in v1:
time: 69.7 us; the launch traced here: 68.6 us
  Pallas kernels  62 us (89%)
  local copies, waits for them, and re-layouts  5.86 us (8%)
    pallas_call x1, Pallas kernels, local(): pl.pallas_call(functools.partial(kernel, lay, owned * lay.n_dom), out_sha...  62 us
    unnamed x14, local copies, waits for them, and re-layouts  5.86 us

profile of v1, /device:TPU:1, one launch (start us, length us, event | category | flops | bytes accessed | tf_op | source)
XLA Modules:
  0.0 68.6 jit_solution(2500952568299032552)
XLA Ops:
  0.6 0.0 copy-start.5
  0.6 0.6 copy-done.5
  1.3 0.0 copy-start
  1.3 0.9 %copy-done = bf16[343,343]{1,0:T(8,128)(2,1)S(1)} copy-done((bf16[343,343]{1,0:T(8,128)(2,1)S(1)}, bf16[343,343]{1,0:T(8,128)(2,1)}, u32[]{:S(2)}) %copy-start) | copy-done | bytes 235322
  2.2 0.0 copy-start.1
  2.2 0.9 %copy-done.1 = f32[8,3072]{1,0:T(8,128)S(1)} copy-done((f32[8,3072]{1,0:T(8,128)S(1)}, f32[8,3072]{1,0:T(8,128)}, u32[]{:S(2)}) %copy-start.1) | copy-done | bytes 98328
  3.1 0.0 copy-start.2
  3.1 0.7 %copy-done.2 = s32[16,343]{1,0:T(8,128)S(1)} copy-done((s32[16,343]{1,0:T(8,128)S(1)}, s32[16,343]{1,0:T(8,128)}, u32[]{:S(2)}) %copy-start.2) | copy-done | bytes 21976
  3.9 0.0 copy-start.3
  3.9 0.7 %copy-done.3 = f32[3072]{0:T(1024)S(1)} copy-done((f32[3072]{0:T(1024)S(1)}, f32[3072]{0:T(1024)}, u32[]{:S(2)}) %copy-start.3) | copy-done | bytes 12312
  4.6 0.0 copy-start.4
  4.6 0.7 %copy-done.4 = f32[3072]{0:T(1024)S(1)} copy-done((f32[3072]{0:T(1024)S(1)}, f32[3072]{0:T(1024)}, u32[]{:S(2)}) %copy-start.4) | copy-done | bytes 12312
  5.3 62.0 %shard_map.77 = (bf16[8,3072]{1,0:T(8,128)(2,1)S(1)}, f32[8,256]{1,0:T(8,128)S(1)}) custom-call(f32[8,3072]{1,0:T(8,128)S(1)} %copy-done.1, s32[16,343]{1,0:T(8,128)S(1)} %copy-done.2, f32[16]{0:T(128)S(1)} %copy-done.5, bf16[343,343]{1,0:T(8,128)(2,1)S(1)} %copy-done, f32[1,3072]{1,0:T(1,128)S(1)} %bitcast.2, f32[1,3072]{1,0:T(1,128)S(1)} %bitcast.3), custom_call_target="tpu_custom_call" | custom-call | tf_op jit(solution)/shard_map/pallas_call | solution.py:302
  67.3 0.6 copy.10
  68.0 0.6 copy.11
Async XLA Ops:
  0.6 0.7 copy-start.5
  1.3 1.0 %copy-start = (bf16[343,343]{1,0:T(8,128)(2,1)S(1)}, bf16[343,343]{1,0:T(8,128)(2,1)}, u32[]{:S(2)}) copy-start(bf16[343,343]{1,0:T(8,128)(2,1)} %matrix.1) | copy-start | bytes 705898
  2.2 0.9 %copy-start.1 = (f32[8,3072]{1,0:T(8,128)S(1)}, f32[8,3072]{1,0:T(8,128)}, u32[]{:S(2)}) copy-start(f32[8,3072]{1,0:T(8,128)} %states.1) | copy-start | bytes 294916
  3.1 0.7 %copy-start.2 = (s32[16,343]{1,0:T(8,128)S(1)}, s32[16,343]{1,0:T(8,128)}, u32[]{:S(2)}) copy-start(s32[16,343]{1,0:T(8,128)} %nodes.1) | copy-start | bytes 65860
  3.9 0.7 %copy-start.3 = (f32[3072]{0:T(1024)S(1)}, f32[3072]{0:T(1024)}, u32[]{:S(2)}) copy-start(f32[3072]{0:T(1024)} %param.10) | copy-start | bytes 36868
  4.6 0.7 %copy-start.4 = (f32[3072]{0:T(1024)S(1)}, f32[3072]{0:T(1024)}, u32[]{:S(2)}) copy-start(f32[3072]{0:T(1024)} %param.11) | copy-start | bytes 36868

commit v2 on v1

--- a/solution.py
+++ b/solution.py
@@ -35,43 +35,50 @@
 class Layout:
     def __init__(self, n_band, n_dom):
         self.n_band, self.n_dom = n_band, n_dom
-        self.nz = 4 if n_band == 32 else 2
-        self.ny = n_band // self.nz
-        self.nx = 8 if n_dom == 24 else 2
-        self.nh = n_dom // self.nx
-        self.per = 24 // self.ny
+        self.ny, self.nz = 8, n_band // 8
 
 
 def kernel(
     lay, nodes_all,
-    states, nodes, cell_scale, matrix, node_scale, potential,
-    filtered, gram,
+    states_hbm, nodes_hbm, scale_hbm, matrix_hbm, node_scale_hbm, potential_hbm,
+    filtered_hbm, gram_hbm,
+    filtered, gram, states, nodes, cell_scale, matrix, node_scale, potential,
     lt, le, mat, pad_nodes, hb, y0, y1, y2, ns, pc, acc, w2, mid, picked, x16, vh,
-    stage, init_in, out_low, out_up, in_low, in_up, shares, got, part, part_in, sum1, sum1_in, sum2, sum2_in,
-    send_sem, recv_sem, gram_send, gram_recv,
+    stage, init_in, out_low, out_up, in_low, in_up, shares, got, got_edge, part, part_in, sums, sums_in,
+    send_sem, recv_sem, gram_send, gram_recv, load_sem, store_sem,
 ):
     band, dom = lax.axis_index("band"), lax.axis_index("dom")
     n_band, n_dom = lay.n_band, lay.n_dom
     left, right = lax.rem(dom + n_dom - 1, n_dom), lax.rem(dom + 1, n_dom)
     my_y, my_z = band // lay.nz, lax.rem(band, lay.nz)
-    my_h, my_x = dom // lay.nx, lax.rem(dom, lay.nx)
     has_left, has_right = dom > 0, dom < n_dom - 1
+    odd = lax.rem(dom, 2)
+
+    loads = [
+        pltpu.make_async_copy(src, dst, load_sem.at[i])
+        for i, (src, dst) in enumerate((
+            (nodes_hbm, nodes), (matrix_hbm, matrix), (states_hbm, states),
+            (node_scale_hbm, node_scale), (potential_hbm, potential), (scale_hbm, cell_scale),
+        ))
+    ]
+    for load in loads:
+        load.start()
 
     band_peers = [lax.rem(band + i, n_band) for i in range(1, n_band)]
-    x_peers = [my_h * lay.nx + lax.rem(my_x + i, lay.nx) for i in range(1, lay.nx)]
-    h_peers = [lax.rem(my_h + i, lay.nh) * lay.nx + my_x for i in range(1, lay.nh)]
-
+    dom_peers = [lax.rem(dom + i, n_dom) for i in range(1, n_dom)]
     barrier = pltpu.get_barrier_semaphore()
-    dom_peers = [left, right] + x_peers + h_peers
     for peer in dom_peers:
         pl.semaphore_signal(barrier, inc=1, device_id=(band, peer), device_id_type=MESH)
     for peer in band_peers:
         pl.semaphore_signal(barrier, inc=1, device_id=(peer, dom), device_id_type=MESH)
+    for load in loads:
+        load.wait()
 
     pad_nodes[...] = jnp.full(pad_nodes.shape, -4096, jnp.int32)
     pad_nodes[:16, :343] = nodes[...]
     mat[...] = jnp.zeros(mat.shape, BF16)
     mat[:343, :343] = matrix[...]
+    mat[...] = mat[...].astype(F32).T.astype(BF16)
     shifted = pad_nodes[...] + 128
     lo_all = shifted & 255
     hi_all = shifted >> 8
@@ -178,27 +185,47 @@
     weigh(y0, upper)
     gather(RIM_HI, False)
 
-    gram_copies = []
+    outer = 7 * odd
+
+    def gram_copy(src, dst, slot, device):
+        pltpu.make_async_remote_copy(
+            src_ref=src, dst_ref=dst, send_sem=gram_send.at[slot], recv_sem=gram_recv.at[slot],
+            device_id=device, device_id_type=MESH,
+        ).start()
+
+    def wait_bytes(ref, send, slot):
+        sem = (gram_send if send else gram_recv).at[slot]
+        pltpu.make_async_copy(ref, ref, sem).wait()
 
     def send_share(share):
         for z in range(lay.nz):
-            def go(share=share, z=z):
-                pltpu.make_async_remote_copy(
-                    src_ref=shares.at[share], dst_ref=got.at[band],
-                    send_sem=gram_send.at[0], recv_sem=gram_recv.at[0],
-                    device_id=(share * lay.nz + z, dom), device_id_type=MESH,
-                ).start()
-            pl.when(band != share * lay.nz + z)(go)
-
-    def fill_shares(which):
-        for share in which:
-            tiles = OWN_TILES[lay.per * share : lay.per * share + lay.per]
-            shares[share] = jnp.concatenate([tile(y1, *t) for t in tiles], axis=1).astype(BF16)
-            filtered[:, 128 * lay.per * share : 128 * lay.per * (share + 1)] = shares[share]
-            send_share(share)
+            to = share * lay.nz + z
+
+            @pl.when(band != to)
+            def _():
+                gram_copy(shares.at[share], got.at[band], 0, (to, dom))
+
+    def fill_share(share):
+        tiles = OWN_TILES[3 * share : 3 * share + 3]
+        value = jnp.concatenate([tile(y1, *t) for t in tiles], axis=1).astype(BF16)
+        shares[share] = value
+        filtered[:, 384 * share : 384 * share + 384] = value
+
+    def finish_edge(copy, low):
+        copy.wait_recv()
+        there, source = (has_left, in_low) if low else (has_right, in_up)
+        for i, t in enumerate(LOW_TILES[3:] if low else UP_TILES[:3]):
+            put(acc, *t, tile(acc, *t) + jnp.where(there, source[2, 8 * i : 8 * i + 8], 0.0))
+        if low:
+            advance(2, slice(16, 24), whole)
+            advance(2, slice(24, 32), slice(0, 128))
+        else:
+            advance(2, slice(96, 104), slice(128, 256))
+            advance(2, slice(104, 112), whole)
+        fill_share(0 if low else 7)
 
     for step in range(3):
-        cells = dot_t(picked[...], mat[...])
+        cells = jnp.dot(picked[...], mat[...], preferred_element_type=F32)
         for p in range(8):
             x = jnp.concatenate(
                 [cells[16 * p : 16 * p + 8] * cell_scale[2 * p],
@@ -222,92 +249,117 @@
         if last:
             advance(step, slice(24, 32), slice(128, 256))
             advance(step, slice(96, 104), slice(0, 128))
-            fill_shares(range(1, lay.ny - 1))
-        else:
-            weigh((y1, y2)[step], middle)
-            gather(MID_HI, True)
+            for share in range(1, 7):
+                fill_share(share)
+            for i in range(6):
+                send_share(1 + i)
+            pl.when(odd == 1)(lambda: finish_edge(now[1], True))
+            pl.when(odd == 0)(lambda: finish_edge(now[0], False))
+            send_share(7 - outer)
+            pl.when(odd == 1)(lambda: finish_edge(now[0], False))
+            pl.when(odd == 0)(lambda: finish_edge(now[1], True))
+            for peer in band_peers:
+                gram_copy(shares.at[outer], got_edge.at[band], 1, (peer, dom))
+            store = pltpu.make_async_copy(filtered, filtered_hbm, store_sem.at[0])
+            store.start()
+            continue
+        weigh((y1, y2)[step], middle)
+        gather(MID_HI, True)
         for copy in now:
             copy.wait_recv()
-        low_to, up_to = (LOW_TILES[3:], UP_TILES[:3]) if last else (LOW_TILES, UP_TILES)
-        for i, (lt_, ut_) in enumerate(zip(low_to, up_to)):
+        for i, (lt_, ut_) in enumerate(zip(LOW_TILES, UP_TILES)):
             got_low = jnp.where(has_left, in_low[step, 8 * i : 8 * i + 8], 0.0)
             got_up = jnp.where(has_right, in_up[step, 8 * i : 8 * i + 8], 0.0)
             put(acc, *lt_, tile(acc, *lt_) + got_low)
             put(acc, *ut_, tile(acc, *ut_) + got_up)
-        if last:
-            advance(step, slice(16, 24), whole)
-            advance(step, slice(24, 32), slice(0, 128))
-            advance(step, slice(96, 104), slice(128, 256))
-            advance(step, slice(104, 112), whole)
-            fill_shares((0, lay.ny - 1))
-        else:
-            advance(step, lower, whole)
-            advance(step, upper, whole)
-            weigh((y1, y2)[step], lower)
-            weigh((y1, y2)[step], upper)
-            gather(RIM_HI, False)
-
-    def wait_bytes(ref, send, slot):
-        sem = (gram_send if send else gram_recv).at[slot]
-        pltpu.make_async_copy(ref, ref, sem).wait()
-
-    got[band] = shares[my_y]
-    wait_bytes(got.at[0 : n_band - 1], False, 0)
-    columns = got[...].astype(F32).reshape(8 * n_band, 128 * lay.per).astype(BF16)
-    rows = jnp.concatenate(
-        [got[y * lay.nz + my_z].astype(F32) for y in range(lay.ny)], axis=0
-    ).astype(BF16)
-    part[...] = dot_t(rows, columns).reshape(lay.ny, 8, 8 * n_band)
-
-    def reduce(peers, src, dst, slot, index, own):
-        for device, piece in peers:
-            pltpu.make_async_remote_copy(
-                src_ref=src(piece), dst_ref=dst.at[index],
-                send_sem=gram_send.at[slot], recv_sem=gram_recv.at[slot],
-                device_id=device, device_id_type=MESH,
-            ).start()
-        dst[index] = own
-        wait_bytes(dst.at[0 : len(peers)], False, slot)
-        total = dst[0]
-        for i in range(1, len(peers) + 1):
-            total = total + dst[i]
-        return total
-
-    y_peers = [lax.rem(my_y + i, lay.ny) for i in range(1, lay.ny)]
-    sum1[...] = reduce(
-        [((y * lay.nz + my_z, dom), y) for y in y_peers],
-        lambda piece: part.at[piece], part_in, 1, my_y, part[my_y],
-    )
-    sum2[...] = reduce(
-        [((band, peer), None) for peer in x_peers], lambda piece: sum1, sum1_in, 2, my_x, sum1[...]
-    )
-    total = reduce(
-        [((band, peer), None) for peer in h_peers], lambda piece: sum2, sum2_in, 3, my_h, sum2[...]
-    )
+        advance(step, lower, whole)
+        advance(step, upper, whole)
+        weigh((y1, y2)[step], lower)
+        weigh((y1, y2)[step], upper)
+        gather(RIM_HI, False)
+
+    def stack(refs):
+        return jnp.concatenate([ref.astype(F32) for ref in refs], axis=0).astype(BF16)
+
+    @pl.when(my_y != outer)
+    def _():
+        got[band] = shares[my_y]
+        wait_bytes(got.at[0 : n_band - 1], False, 0)
+        columns = got[...].astype(F32).reshape(8 * n_band, 384).astype(BF16)
+        rows = stack([got[y * lay.nz + my_z] for y in range(lay.ny)])
+        part[...] = dot_t(rows, columns).reshape(lay.ny, 8, 8 * n_band)
+        for i in range(1, lay.ny):
+            y = lax.rem(my_y + i, lay.ny)
+            gram_copy(part.at[y], part_in.at[my_y], 2, (y * lay.nz + my_z, dom))
+        part_in[my_y] = part[my_y]
+        part_in[outer] = jnp.zeros((8, 8 * n_band), F32)
+        wait_bytes(part_in.at[0 : lay.ny - 2], False, 2)
+
+    @pl.when(my_y == outer)
+    def _():
+        part_in[outer] = jnp.zeros((8, 8 * n_band), F32)
+        wait_bytes(part_in.at[0 : lay.ny - 1], False, 2)
+
+    total = part_in[0]
+    for i in range(1, lay.ny):
+        total = total + part_in[i]
+
+    got_edge[band] = shares[outer]
+    wait_bytes(got_edge.at[0 : n_band - 1], False, 1)
+    columns = got_edge[...].astype(F32).reshape(8 * n_band, 384).astype(BF16)
+    sums[...] = total + dot_t(shares[outer], columns)
+
+    for peer in dom_peers:
+        gram_copy(sums, sums_in.at[dom], 3, (band, peer))
+    sums_in[dom] = sums[...]
+    wait_bytes(sums_in.at[0 : n_dom - 1], False, 3)
+    total = sums_in[0]
+    for i in range(1, n_dom):
+        total = total + sums_in[i]
     gram[...] = total * (1.0 / nodes_all)
+    store_gram = pltpu.make_async_copy(gram, gram_hbm, store_sem.at[1])
+    store_gram.start()
 
     for copy in started:
         copy.wait_send()
-    wait_bytes(got.at[0 : n_band - 1], True, 0)
-    wait_bytes(part_in.at[0 : lay.ny - 1], True, 1)
-    wait_bytes(sum1_in.at[0 : lay.nx - 1], True, 2)
-    wait_bytes(sum2_in.at[0 : lay.nh - 1], True, 3)
+
+    @pl.when(my_y != outer)
+    def _():
+        wait_bytes(got.at[0 : 7 * lay.nz - 1], True, 0)
+        wait_bytes(part_in.at[0 : lay.ny - 1], True, 2)
+
+    @pl.when(my_y == outer)
+    def _():
+        wait_bytes(got.at[0 : 7 * lay.nz], True, 0)
+
+    wait_bytes(got_edge.at[0 : n_band - 1], True, 1)
+    wait_bytes(sums_in.at[0 : n_dom - 1], True, 3)
+    store.wait()
+    store_gram.wait()
 
 
 def local(lay, states_in, cell_nodes, cell_scale, cell_matrix, node_scale, potential):
     owned = states_in.shape[1]
     cells = cell_nodes.shape[0] * 384
-    vmem, smem = pl.BlockSpec(memory_space=pltpu.VMEM), pl.BlockSpec(memory_space=pltpu.SMEM)
-    n_band, share = lay.n_band, 128 * lay.per
+    hbm = pl.BlockSpec(memory_space=pltpu.HBM)
+    n_band = lay.n_band
     return pl.pallas_call(
         functools.partial(kernel, lay, owned * lay.n_dom),
         out_shape=(
             jax.ShapeDtypeStruct((8, owned), BF16),
             jax.ShapeDtypeStruct((8, 8 * n_band), F32),
         ),
-        in_specs=[vmem, vmem, smem, vmem, vmem, vmem],
-        out_specs=(vmem, vmem),
+        in_specs=[hbm] * 6,
+        out_specs=(hbm, hbm),
         scratch_shapes=[
+            pltpu.VMEM((8, owned), BF16),
+            pltpu.VMEM((8, 8 * n_band), F32),
+            pltpu.VMEM(states_in.shape, F32),
+            pltpu.VMEM(cell_nodes.shape, jnp.int32),
+            pltpu.SMEM(cell_scale.shape, F32),
+            pltpu.VMEM(cell_matrix.shape, BF16),
+            pltpu.VMEM((1, owned), F32),
+            pltpu.VMEM((1, owned), F32),
             pltpu.VMEM((256, cells), BF16),
             pltpu.VMEM((cells, 256), BF16),
             pltpu.VMEM((384, 384), BF16),
@@ -330,21 +382,22 @@
             pltpu.VMEM((3, 48, 128), F32),
             pltpu.VMEM((3, 48, 128), F32),
             pltpu.VMEM((3, 48, 128), F32),
-            pltpu.VMEM((lay.ny, 8, share), BF16),
-            pltpu.VMEM((n_band, 8, share), BF16),
+            pltpu.VMEM((8, 8, 384), BF16),
+            pltpu.VMEM((n_band, 8, 384), BF16),
+            pltpu.VMEM((n_band, 8, 384), BF16),
             pltpu.VMEM((lay.ny, 8, 8 * n_band), F32),
             pltpu.VMEM((lay.ny, 8, 8 * n_band), F32),
             pltpu.VMEM((8, 8 * n_band), F32),
-            pltpu.VMEM((lay.nx, 8, 8 * n_band), F32),
-            pltpu.VMEM((8, 8 * n_band), F32),
-            pltpu.VMEM((lay.nh, 8, 8 * n_band), F32),
+            pltpu.VMEM((lay.n_dom, 8, 8 * n_band), F32),
             pltpu.SemaphoreType.DMA((8,)),
             pltpu.SemaphoreType.DMA((8,)),
             pltpu.SemaphoreType.DMA((4,)),
             pltpu.SemaphoreType.DMA((4,)),
+            pltpu.SemaphoreType.DMA((6,)),
+            pltpu.SemaphoreType.DMA((2,)),
         ],
         compiler_params=pltpu.CompilerParams(
-            collective_id=0, has_side_effects=True, vmem_limit_bytes=48 * 1024 * 1024
+            collective_id=0, has_side_effects=True, vmem_limit_bytes=60 * 1024 * 1024
         ),
     )(states_in, cell_nodes, cell_scale, cell_matrix, node_scale[None, :], potential[None, :])
 

time: 69.7 us -> 67 us (0.961); the launches traced: 68.6 us -> 66.8 us
  local copies, waits for them, and re-layouts: 5.86 us -> 2.03 us
  Pallas kernels: 62 us -> 64.1 us
    unnamed x14 -> x4, local copies, waits for them, and re-layouts: 5.86 us -> 2.03 us
    pallas_call x1, Pallas kernels: 62 us -> 64.1 us  [local(): pl.pallas_call(functools.partial(kernel, lay, owned * lay.n_dom), out_sha...]
where the time goes in v2:
time: 67 us; the launch traced here: 66.8 us
  Pallas kernels  64.1 us (96%)
  local copies, waits for them, and re-layouts  2.03 us (3%)
    pallas_call x1, Pallas kernels, local(): pl.pallas_call(functools.partial(kernel, lay, owned * lay.n_dom), out_sha...  64.1 us
    unnamed x4, local copies, waits for them, and re-layouts  2.03 us

profile of v2, /device:TPU:1, one launch (start us, length us, event | category | flops | bytes accessed | tf_op | source)
XLA Modules:
  0.0 66.8 jit_solution(5964587676657746840)
XLA Ops:
  0.6 64.1 %shard_map.77 = (bf16[8,3072]{1,0:T(8,128)(2,1)}, f32[8,256]{1,0:T(8,128)}) custom-call(f32[8,3072]{1,0:T(8,128)} %states_hbm.1, s32[16,343]{1,0:T(8,128)} %nodes_hbm.1, f32[16]{0:T(128)} %scale_hbm.1, bf16[343,343]{1,0:T(8,128)(2,1)} %matrix_hbm.1, f32[1,3072]{1,0:T(1,128)} %bitcast.2, f32[1,3072]{1,0:T(1,128)} %bitcast.3), custom_call_target="tpu_custom_call" | custom-call | tf_op jit(solution)/shard_map/pallas_call | solution.py:346
  64.8 0.0 copy-start
  64.8 1.4 %copy.10 = bf16[8,3072]{1,0:T(8,128)(2,1)} copy(bf16[8,3072]{1,0:T(8,128)(2,1)} %get-tuple-element.4) | data formatting | bytes 98304
  66.2 0.0 copy-done
  66.2 0.6 copy.11
Async XLA Ops:
  64.8 1.4 %copy-start = (f32[8,256]{1,0:T(8,128)S(1)}, f32[8,256]{1,0:T(8,128)}, u32[]{:S(2)}) copy-start(f32[8,256]{1,0:T(8,128)} %get-tuple-element.5) | copy-start | bytes 24580

commit v3 on v2

--- a/solution.py
+++ b/solution.py
@@ -14,6 +14,7 @@
 BF16 = jnp.bfloat16
 
 RIM_HI = (0, 1, 2, 3, 12, 13, 14, 15)
+RIM_TILES = tuple((t // 2, t % 2) for t in (*range(1, 8), *range(24, 31)))
 MID_HI = (4, 5, 6, 7, 8, 9, 10, 11)
 LOW_TILES = ((0, 1), (1, 0), (1, 1), (2, 0), (2, 1), (3, 0))
 UP_TILES = ((12, 1), (13, 0), (13, 1), (14, 0), (14, 1), (15, 0))
@@ -43,7 +44,7 @@
     states_hbm, nodes_hbm, scale_hbm, matrix_hbm, node_scale_hbm, potential_hbm,
     filtered_hbm, gram_hbm,
     filtered, gram, states, nodes, cell_scale, matrix, node_scale, potential,
-    lt, le, mat, pad_nodes, hb, y0, y1, y2, ns, pc, acc, w2, mid, picked, x16, vh,
+    lt, lt_half, le, mat, pad_nodes, hb, hb_half, y0, y1, y2, ns, pc, acc, w1, w2, mid, x16, vh,
     stage, init_in, out_low, out_up, in_low, in_up, shares, got, got_edge, part, part_in, sums, sums_in,
     send_sem, recv_sem, gram_send, gram_recv, load_sem, store_sem,
 ):
@@ -54,6 +55,14 @@
     has_left, has_right = dom > 0, dom < n_dom - 1
     odd = lax.rem(dom, 2)
 
+    band_peers = [lax.rem(band + i, n_band) for i in range(1, n_band)]
+    order = [i for i in (n_dom - 1, *range(1, n_dom - 1))]
+    dom_peers = [lax.rem(dom + i, n_dom) for i in order]
+    barrier = pltpu.get_barrier_semaphore()
+    for peer in dom_peers:
+        pl.semaphore_signal(barrier, inc=1, device_id=(band, peer), device_id_type=MESH)
+    for peer in band_peers:
+        pl.semaphore_signal(barrier, inc=1, device_id=(peer, dom), device_id_type=MESH)
     loads = [
         pltpu.make_async_copy(src, dst, load_sem.at[i])
         for i, (src, dst) in enumerate((
@@ -63,14 +72,6 @@
     ]
     for load in loads:
         load.start()
-
-    band_peers = [lax.rem(band + i, n_band) for i in range(1, n_band)]
-    dom_peers = [lax.rem(dom + i, n_dom) for i in range(1, n_dom)]
-    barrier = pltpu.get_barrier_semaphore()
-    for peer in dom_peers:
-        pl.semaphore_signal(barrier, inc=1, device_id=(band, peer), device_id_type=MESH)
-    for peer in band_peers:
-        pl.semaphore_signal(barrier, inc=1, device_id=(peer, dom), device_id_type=MESH)
     for load in loads:
         load.wait()
 
@@ -90,7 +91,9 @@
         lo = jnp.concatenate([lo_all[2 * p : 2 * p + 1], lo_all[2 * p + 1 : 2 * p + 2]], axis=1)
         hi = jnp.concatenate([hi_all[2 * p : 2 * p + 1], hi_all[2 * p + 1 : 2 * p + 2]], axis=1)
         hb[p] = jnp.broadcast_to(hi, (8, 768))
+        hb_half[p] = jnp.broadcast_to(2 * hi + (lo >> 7), (8, 768))
         lt[:, cols] = jnp.where(row_iota == lo, 1.0, 0.0).astype(BF16)
+        lt_half[:, cols] = jnp.where(row_iota[:128] == (lo & 127), 1.0, 0.0).astype(BF16)
         for c in (2 * p, 2 * p + 1):
             le[384 * c : 384 * c + 384, :] = jnp.where(
                 lane_iota == lo_t[:, c : c + 1], 1.0, 0.0
@@ -125,36 +128,59 @@
         rim_copy(stage.at[1], init_in.at[0], 1, right),
     ]
 
-    def gather(his, first):
-        runs = [(his[0], his[-1] + 1)] if his == MID_HI else [(0, 4), (12, 16)]
-        left_side = jnp.concatenate([w2[8 * a : 8 * b, :] for a, b in runs], axis=0)
+    def gather_mid():
         for p in range(8):
             cols = slice(768 * p, 768 * p + 768)
-            t = jnp.dot(left_side, lt[:, cols], preferred_element_type=F32)
+            t = jnp.dot(w2[...], lt[:, cols], preferred_element_type=F32)
             index = hb[p]
-            total = jnp.zeros((8, 768), F32) if first else mid[:, cols]
-            for k, hi in enumerate(his):
+            total = jnp.zeros((8, 768), F32)
+            for k, hi in enumerate(MID_HI):
                 total = jnp.where(index == hi, t[8 * k : 8 * k + 8], total)
-            if first:
-                mid[:, cols] = total
-            else:
-                picked[16 * p : 16 * p + 16, :] = jnp.concatenate(
-                    [total[:, :384], total[:, 384:]], axis=0
-                ).astype(BF16)
-
-    def scatter(his):
-        for p in range(8):
-            cols = slice(768 * p, 768 * p + 768)
-            index = jnp.concatenate([hb[p], hb[p]], axis=0)
-            x = x16[:, cols]
-            for k, hi in enumerate(his):
-                vh[16 * k : 16 * k + 16, cols] = jnp.where(index == hi, x, 0.0).astype(BF16)
-        r = jnp.dot(vh[...], le[...], preferred_element_type=F32)
+            mid[:, cols] = total
+
+    def gather_rim(p):
+        cols = slice(768 * p, 768 * p + 768)
+        t = jnp.dot(w1[...], lt_half[:, cols], preferred_element_type=F32)
+        index = hb_half[p]
+        total = mid[:, cols]
+        for k, (hi, half) in enumerate(RIM_TILES):
+            total = jnp.where(index == 2 * hi + half, t[8 * k : 8 * k + 8], total)
+        return [total[:, :384], total[:, 384:]]
+
+    def spread(his, p, x):
+        cols = slice(768 * p, 768 * p + 768)
+        index = jnp.concatenate([hb[p], hb[p]], axis=0)
+        for k, hi in enumerate(his):
+            vh[16 * k : 16 * k + 16, cols] = jnp.where(index == hi, x, 0.0).astype(BF16)
+
+    def collect(his, r):
         for k, hi in enumerate(his):
             acc[8 * hi : 8 * hi + 8, :] = r[16 * k : 16 * k + 8] + r[16 * k + 8 : 16 * k + 16]
 
-    def weigh(y, rows):
-        w2[rows, :] = (ns[rows, :] * y[rows, :]).astype(BF16)
+    def rim_pass():
+        values = jnp.concatenate([v for p in range(8) for v in gather_rim(p)], axis=0).astype(BF16)
+        cells = jnp.dot(values, mat[...], preferred_element_type=F32)
+        for p in range(8):
+            x = jnp.concatenate(
+                [cells[16 * p : 16 * p + 8] * cell_scale[2 * p],
+                 cells[16 * p + 8 : 16 * p + 16] * cell_scale[2 * p + 1]], axis=1)
+            x = jnp.concatenate([x, x - x.astype(BF16).astype(F32)], axis=0)
+            x16[:, 768 * p : 768 * p + 768] = x
+            spread(RIM_HI, p, x)
+        collect(RIM_HI, jnp.dot(vh[...], le[...], preferred_element_type=F32))
+
+    def scatter_mid():
+        for p in range(8):
+            spread(MID_HI, p, x16[:, 768 * p : 768 * p + 768])
+        collect(MID_HI, jnp.dot(vh[...], le[...], preferred_element_type=F32))
+
+    def weigh_mid(y):
+        w2[...] = (ns[32:96] * y[32:96]).astype(BF16)
+
+    def weigh_rim(y):
+        for i in range(0, len(RIM_TILES), 2):
+            pair = [tile(ns, *t) * tile(y, *t) for t in RIM_TILES[i : i + 2]]
+            w1[8 * i : 8 * i + 16, :] = jnp.concatenate(pair, axis=0).astype(BF16)
 
     def advance(step, rows, cols):
         now = (y0, y1, y2)[step][rows, cols]
@@ -169,8 +195,8 @@
     whole = slice(0, 256)
     middle, lower, upper = slice(32, 96), slice(0, 32), slice(96, 128)
 
-    weigh(y0, middle)
-    gather(MID_HI, True)
+    weigh_mid(y0)
+    gather_mid()
     for copy in started:
         copy.wait_recv()
     for side, tiles in ((0, LOW_TILES[:3]), (1, UP_TILES[3:])):
@@ -181,9 +207,7 @@
             put(y0, hi, half, value[0:8, cols])
             put(ns, hi, half, jnp.broadcast_to(value[8:9, cols], (8, 128)))
             put(pc, hi, half, jnp.broadcast_to(value[9:10, cols] - CENTER, (8, 128)))
-    weigh(y0, lower)
-    weigh(y0, upper)
-    gather(RIM_HI, False)
+    weigh_rim(y0)
 
     outer = 7 * odd
 
@@ -225,14 +249,7 @@
         fill_share(0 if low else 7)
 
     for step in range(3):
-        cells = jnp.dot(picked[...], mat[...], preferred_element_type=F32)
-        for p in range(8):
-            x = jnp.concatenate(
-                [cells[16 * p : 16 * p + 8] * cell_scale[2 * p],
-                 cells[16 * p + 8 : 16 * p + 16] * cell_scale[2 * p + 1]], axis=1)
-            rest = x - x.astype(BF16).astype(F32)
-            x16[:, 768 * p : 768 * p + 768] = jnp.concatenate([x, rest], axis=0)
-        scatter(RIM_HI)
+        rim_pass()
         last = step == 2
         low_tiles, up_tiles = (LOW_TILES[:3], UP_TILES[3:]) if last else (LOW_TILES, UP_TILES)
         for i, (lt_, ut_) in enumerate(zip(low_tiles, up_tiles)):
@@ -244,7 +261,7 @@
             rim_copy(out_up.at[step, 0:rows], in_low.at[step, 0:rows], 3 + 2 * step, right),
         ]
         started += now
-        scatter(MID_HI)
+        scatter_mid()
         advance(step, middle, whole)
         if last:
             advance(step, slice(24, 32), slice(128, 256))
@@ -263,8 +280,8 @@
             store = pltpu.make_async_copy(filtered, filtered_hbm, store_sem.at[0])
             store.start()
             continue
-        weigh((y1, y2)[step], middle)
-        gather(MID_HI, True)
+        weigh_mid((y1, y2)[step])
+        gather_mid()
         for copy in now:
             copy.wait_recv()
         for i, (lt_, ut_) in enumerate(zip(LOW_TILES, UP_TILES)):
@@ -274,9 +291,7 @@
             put(acc, *ut_, tile(acc, *ut_) + got_up)
         advance(step, lower, whole)
         advance(step, upper, whole)
-        weigh((y1, y2)[step], lower)
-        weigh((y1, y2)[step], upper)
-        gather(RIM_HI, False)
+        weigh_rim((y1, y2)[step])
 
     def stack(refs):
         return jnp.concatenate([ref.astype(F32) for ref in refs], axis=0).astype(BF16)
@@ -307,15 +322,13 @@
     got_edge[band] = shares[outer]
     wait_bytes(got_edge.at[0 : n_band - 1], False, 1)
     columns = got_edge[...].astype(F32).reshape(8 * n_band, 384).astype(BF16)
-    sums[...] = total + dot_t(shares[outer], columns)
+    sums[...] = (total + dot_t(shares[outer], columns)).astype(BF16)
 
     for peer in dom_peers:
         gram_copy(sums, sums_in.at[dom], 3, (band, peer))
     sums_in[dom] = sums[...]
     wait_bytes(sums_in.at[0 : n_dom - 1], False, 3)
-    total = sums_in[0]
-    for i in range(1, n_dom):
-        total = total + sums_in[i]
+    total = jnp.sum(sums_in[...].astype(F32), axis=0)
     gram[...] = total * (1.0 / nodes_all)
     store_gram = pltpu.make_async_copy(gram, gram_hbm, store_sem.at[1])
     store_gram.start()
@@ -336,6 +349,17 @@
     wait_bytes(sums_in.at[0 : n_dom - 1], True, 3)
     store.wait()
     store_gram.wait()
+
+
+def hand_over(filtered_from, gram_from, filtered, gram, sem):
+    copies = [
+        pltpu.make_async_copy(filtered_from, filtered, sem.at[0]),
+        pltpu.make_async_copy(gram_from, gram, sem.at[1]),
+    ]
+    for copy in copies:
+        copy.start()
+    for copy in copies:
+        copy.wait()
 
 
 def local(lay, states_in, cell_nodes, cell_scale, cell_matrix, node_scale, potential):
@@ -343,12 +367,13 @@
     cells = cell_nodes.shape[0] * 384
     hbm = pl.BlockSpec(memory_space=pltpu.HBM)
     n_band = lay.n_band
-    return pl.pallas_call(
+    out_shape = (
+        jax.ShapeDtypeStruct((8, owned), BF16),
+        jax.ShapeDtypeStruct((8, 8 * n_band), F32),
+    )
+    results = pl.pallas_call(
         functools.partial(kernel, lay, owned * lay.n_dom),
-        out_shape=(
-            jax.ShapeDtypeStruct((8, owned), BF16),
-            jax.ShapeDtypeStruct((8, 8 * n_band), F32),
-        ),
+        out_shape=out_shape,
         in_specs=[hbm] * 6,
         out_specs=(hbm, hbm),
         scratch_shapes=[
@@ -361,19 +386,21 @@
             pltpu.VMEM((1, owned), F32),
             pltpu.VMEM((1, owned), F32),
             pltpu.VMEM((256, cells), BF16),
+            pltpu.VMEM((128, cells), BF16),
             pltpu.VMEM((cells, 256), BF16),
             pltpu.VMEM((384, 384), BF16),
             pltpu.VMEM((128, 384), jnp.int32),
             pltpu.VMEM((8, 8, 768), jnp.int32),
-            pltpu.VMEM((128, 256), F32),
-            pltpu.VMEM((128, 256), F32),
-            pltpu.VMEM((128, 256), F32),
-            pltpu.VMEM((128, 256), F32),
-            pltpu.VMEM((128, 256), F32),
-            pltpu.VMEM((128, 256), F32),
-            pltpu.VMEM((128, 256), BF16),
+            pltpu.VMEM((8, 8, 768), jnp.int32),
+            pltpu.VMEM((128, 256), F32),
+            pltpu.VMEM((128, 256), F32),
+            pltpu.VMEM((128, 256), F32),
+            pltpu.VMEM((128, 256), F32),
+            pltpu.VMEM((128, 256), F32),
+            pltpu.VMEM((128, 256), F32),
+            pltpu.VMEM((112, 128), BF16),
+            pltpu.VMEM((64, 256), BF16),
             pltpu.VMEM((8, cells), F32),
-            pltpu.VMEM((128, 384), BF16),
             pltpu.VMEM((16, cells), F32),
             pltpu.VMEM((128, cells), BF16),
             pltpu.VMEM((2, 16, 384), F32),
@@ -387,8 +414,8 @@
             pltpu.VMEM((n_band, 8, 384), BF16),
             pltpu.VMEM((lay.ny, 8, 8 * n_band), F32),
             pltpu.VMEM((lay.ny, 8, 8 * n_band), F32),
-            pltpu.VMEM((8, 8 * n_band), F32),
-            pltpu.VMEM((lay.n_dom, 8, 8 * n_band), F32),
+            pltpu.VMEM((8, 8 * n_band), BF16),
+            pltpu.VMEM((lay.n_dom, 8, 8 * n_band), BF16),
             pltpu.SemaphoreType.DMA((8,)),
             pltpu.SemaphoreType.DMA((8,)),
             pltpu.SemaphoreType.DMA((4,)),
@@ -400,6 +427,11 @@
             collective_id=0, has_side_effects=True, vmem_limit_bytes=60 * 1024 * 1024
         ),
     )(states_in, cell_nodes, cell_scale, cell_matrix, node_scale[None, :], potential[None, :])
+    return pl.pallas_call(
+        hand_over, out_shape=out_shape, in_specs=[hbm] * 2, out_specs=(hbm, hbm),
+        scratch_shapes=[pltpu.SemaphoreType.DMA((2,))],
+        compiler_params=pltpu.CompilerParams(vmem_limit_bytes=60 * 1024 * 1024),
+    )(*results)
 
 
 def solution(mesh):

time: 67 us -> 65.6 us (0.979)
  local copies, waits for them, and re-layouts: 2.03 us -> 0 us
  Pallas kernels: 64.1 us -> 64.8 us
    pallas_call x0 -> x1, Pallas kernels: none -> 2.86 us  [local(): pl.pallas_call(hand_over, out_shape=out_shape, in_specs=[hbm] * 2, out_sp...]
    pallas_call x1, Pallas kernels: 64.1 us -> 61.9 us  [local(): pl.pallas_call(functools.partial(kernel, lay, owned * lay.n_dom), out_sha...]
    unnamed x4 -> x0, local copies, waits for them, and re-layouts: 2.03 us -> none
where the time goes in v3:
time: 65.6 us; the launch traced here: 65.4 us
  Pallas kernels  64.8 us (99%)
    pallas_call x1, Pallas kernels, local(): pl.pallas_call(functools.partial(kernel, lay, owned * lay.n_dom), out_sha...  61.9 us
    pallas_call x1, Pallas kernels, local(): pl.pallas_call(hand_over, out_shape=out_shape, in_specs=[hbm] * 2, out_sp...  2.86 us

profile of v3, /device:TPU:1, one launch (start us, length us, event | category | flops | bytes accessed | tf_op | source)
XLA Modules:
  0.0 65.4 jit_solution(6125881250270394751)
XLA Ops:
  0.6 61.9 %shard_map.77 = (bf16[8,3072]{1,0:T(8,128)(2,1)}, f32[8,256]{1,0:T(8,128)}) custom-call(f32[8,3072]{1,0:T(8,128)} %states_hbm.1, s32[16,343]{1,0:T(8,128)} %nodes_hbm.1, f32[16]{0:T(128)} %scale_hbm.1, bf16[343,343]{1,0:T(8,128)(2,1)} %matrix_hbm.1, f32[1,3072]{1,0:T(1,128)} %bitcast.2, f32[1,3072]{1,0:T(1,128)} %bitcast.3), custom_call_target="tpu_custom_call" | custom-call | tf_op jit(solution)/shard_map/pallas_call | solution.py:374
  62.6 2.9 %shard_map.78 = (bf16[8,3072]{1,0:T(8,128)(2,1)}, f32[8,256]{1,0:T(8,128)}) custom-call(bf16[8,3072]{1,0:T(8,128)(2,1)} %get-tuple-element.4.filtered_from, f32[8,256]{1,0:T(8,128)} %get-tuple-element.5.gram_from), custom_call_target="tpu_custom_call" | custom-call | tf_op jit(solution)/shard_map/pallas_call | solution.py:430

commit v4 on v3

--- a/solution.py
+++ b/solution.py
@@ -55,7 +55,10 @@
     has_left, has_right = dom > 0, dom < n_dom - 1
     odd = lax.rem(dom, 2)
 
-    band_peers = [lax.rem(band + i, n_band) for i in range(1, n_band)]
+    band_peers = [
+        lax.rem(my_y + dy, lay.ny) * lay.nz + lax.rem(my_z + dz, lay.nz)
+        for dy in (4, 3, 5, 2, 6, 1, 7, 0) for dz in range(lay.nz) if dy or dz
+    ]
     order = [i for i in (n_dom - 1, *range(1, n_dom - 1))]
     dom_peers = [lax.rem(dom + i, n_dom) for i in order]
     barrier = pltpu.get_barrier_semaphore()
@@ -268,8 +271,9 @@
             advance(step, slice(96, 104), slice(0, 128))
             for share in range(1, 7):
                 fill_share(share)
-            for i in range(6):
-                send_share(1 + i)
+            for dy in (4, 3, 5, 2, 6, 1, 7, 0):
+                share = lax.rem(my_y + dy, lay.ny)
+                pl.when(jnp.logical_and(share > 0, share < 7))(functools.partial(send_share, share))
             pl.when(odd == 1)(lambda: finish_edge(now[1], True))
             pl.when(odd == 0)(lambda: finish_edge(now[0], False))
             send_share(7 - outer)
@@ -324,8 +328,8 @@
     columns = got_edge[...].astype(F32).reshape(8 * n_band, 384).astype(BF16)
     sums[...] = (total + dot_t(shares[outer], columns)).astype(BF16)
 
-    for peer in dom_peers:
-        gram_copy(sums, sums_in.at[dom], 3, (band, peer))
+    for i in sorted(range(1, n_dom), key=lambda i: -min(i, n_dom - i)):
+        gram_copy(sums, sums_in.at[dom], 3, (band, lax.rem(dom + i, n_dom)))
     sums_in[dom] = sums[...]
     wait_bytes(sums_in.at[0 : n_dom - 1], False, 3)
     total = jnp.sum(sums_in[...].astype(F32), axis=0)
@@ -349,17 +353,6 @@
     wait_bytes(sums_in.at[0 : n_dom - 1], True, 3)
     store.wait()
     store_gram.wait()
-
-
-def hand_over(filtered_from, gram_from, filtered, gram, sem):
-    copies = [
-        pltpu.make_async_copy(filtered_from, filtered, sem.at[0]),
-        pltpu.make_async_copy(gram_from, gram, sem.at[1]),
-    ]
-    for copy in copies:
-        copy.start()
-    for copy in copies:
-        copy.wait()
 
 
 def local(lay, states_in, cell_nodes, cell_scale, cell_matrix, node_scale, potential):
@@ -371,7 +364,7 @@
         jax.ShapeDtypeStruct((8, owned), BF16),
         jax.ShapeDtypeStruct((8, 8 * n_band), F32),
     )
-    results = pl.pallas_call(
+    return pl.pallas_call(
         functools.partial(kernel, lay, owned * lay.n_dom),
         out_shape=out_shape,
         in_specs=[hbm] * 6,
@@ -427,11 +420,6 @@
             collective_id=0, has_side_effects=True, vmem_limit_bytes=60 * 1024 * 1024
         ),
     )(states_in, cell_nodes, cell_scale, cell_matrix, node_scale[None, :], potential[None, :])
-    return pl.pallas_call(
-        hand_over, out_shape=out_shape, in_specs=[hbm] * 2, out_specs=(hbm, hbm),
-        scratch_shapes=[pltpu.SemaphoreType.DMA((2,))],
-        compiler_params=pltpu.CompilerParams(vmem_limit_bytes=60 * 1024 * 1024),
-    )(*results)
 
 
 def solution(mesh):

time: 65.6 us -> 64.2 us (0.979)
  Pallas kernels: 64.8 us -> 61.3 us
  local copies, waits for them, and re-layouts: 0 us -> 2.03 us
    pallas_call x1 -> x0, Pallas kernels: 2.86 us -> none  [local(): pl.pallas_call(hand_over, out_shape=out_shape, in_specs=[hbm] * 2, out_sp...]
    unnamed x0 -> x4, local copies, waits for them, and re-layouts: none -> 2.03 us
where the time goes in v4:
time: 64.2 us; the launch traced here: 64 us
  Pallas kernels  61.3 us (95%)
  local copies, waits for them, and re-layouts  2.03 us (3%)
  between operations  0.65 us (1%)
    pallas_call x1, Pallas kernels, local(): pl.pallas_call(functools.partial(kernel, lay, owned * lay.n_dom), out_sha...  61.3 us
    unnamed x4, local copies, waits for them, and re-layouts  2.03 us

profile of v4, /device:TPU:1, one launch (start us, length us, event | category | flops | bytes accessed | tf_op | source)
XLA Modules:
  0.0 64.0 jit_solution(8005441007328329497)
XLA Ops:
  0.6 61.3 %shard_map.77 = (bf16[8,3072]{1,0:T(8,128)(2,1)}, f32[8,256]{1,0:T(8,128)}) custom-call(f32[8,3072]{1,0:T(8,128)} %states_hbm.1, s32[16,343]{1,0:T(8,128)} %nodes_hbm.1, f32[16]{0:T(128)} %scale_hbm.1, bf16[343,343]{1,0:T(8,128)(2,1)} %matrix_hbm.1, f32[1,3072]{1,0:T(1,128)} %bitcast.2, f32[1,3072]{1,0:T(1,128)} %bitcast.3), custom_call_target="tpu_custom_call" | custom-call | tf_op jit(solution)/shard_map/pallas_call | solution.py:367
  61.9 0.0 copy-start
  61.9 1.4 %copy.10 = bf16[8,3072]{1,0:T(8,128)(2,1)} copy(bf16[8,3072]{1,0:T(8,128)(2,1)} %get-tuple-element.4) | data formatting | bytes 98304
  63.4 0.0 copy-done
  63.4 0.6 copy.11
Async XLA Ops:
  61.9 1.4 %copy-start = (f32[8,256]{1,0:T(8,128)S(1)}, f32[8,256]{1,0:T(8,128)}, u32[]{:S(2)}) copy-start(f32[8,256]{1,0:T(8,128)} %get-tuple-element.5) | copy-start | bytes 24580

commit v5 on v4

--- a/solution.py
+++ b/solution.py
@@ -123,13 +123,24 @@
             src_ref=src, dst_ref=dst, send_sem=send_sem.at[slot], recv_sem=recv_sem.at[slot],
             device_id=(band, to), device_id_type=MESH,
         )
-        copy.start()
         return copy
+
+    def start_both(to_left, to_right):
+        @pl.when(odd == 1)
+        def _():
+            to_right.start()
+            to_left.start()
+
+        @pl.when(odd == 0)
+        def _():
+            to_left.start()
+            to_right.start()
 
     started = [
         rim_copy(stage.at[0], init_in.at[1], 0, left),
         rim_copy(stage.at[1], init_in.at[0], 1, right),
     ]
+    start_both(*started)
 
     def gather_mid():
         for p in range(8):
@@ -234,8 +245,8 @@
 
     def fill_share(share):
         tiles = OWN_TILES[3 * share : 3 * share + 3]
-        value = jnp.concatenate([tile(y1, *t) for t in tiles], axis=1).astype(BF16)
-        shares[share] = value
+        value = jnp.concatenate([tile(y1, *t) for t in tiles], axis=1)
+        shares[share] = value.astype(BF16)
         filtered[:, 384 * share : 384 * share + 384] = value
 
     def finish_edge(copy, low):
@@ -263,6 +274,7 @@
             rim_copy(out_low.at[step, 0:rows], in_up.at[step, 0:rows], 2 + 2 * step, left),
             rim_copy(out_up.at[step, 0:rows], in_low.at[step, 0:rows], 3 + 2 * step, right),
         ]
+        start_both(*now)
         started += now
         scatter_mid()
         advance(step, middle, whole)
@@ -361,16 +373,16 @@
     hbm = pl.BlockSpec(memory_space=pltpu.HBM)
     n_band = lay.n_band
     out_shape = (
-        jax.ShapeDtypeStruct((8, owned), BF16),
+        jax.ShapeDtypeStruct((8, owned), F32),
         jax.ShapeDtypeStruct((8, 8 * n_band), F32),
     )
-    return pl.pallas_call(
+    last, gram = pl.pallas_call(
         functools.partial(kernel, lay, owned * lay.n_dom),
         out_shape=out_shape,
         in_specs=[hbm] * 6,
         out_specs=(hbm, hbm),
         scratch_shapes=[
-            pltpu.VMEM((8, owned), BF16),
+            pltpu.VMEM((8, owned), F32),
             pltpu.VMEM((8, 8 * n_band), F32),
             pltpu.VMEM(states_in.shape, F32),
             pltpu.VMEM(cell_nodes.shape, jnp.int32),
@@ -420,6 +432,7 @@
             collective_id=0, has_side_effects=True, vmem_limit_bytes=60 * 1024 * 1024
         ),
     )(states_in, cell_nodes, cell_scale, cell_matrix, node_scale[None, :], potential[None, :])
+    return last.astype(BF16), gram
 
 
 def solution(mesh):

time: 64.2 us -> 64.8 us (level)
  other arithmetic: 0 us -> 1.52 us
  local copies, waits for them, and re-layouts: 2.03 us -> 0.6 us
    convert_element_type x0 -> x1, other arithmetic: none -> 1.52 us  [local(): return (last.astype(BF16), gram)]
    unnamed x4 -> x3, local copies, waits for them, and re-layouts: 2.03 us -> 0.6 us
where the time goes in v5:
time: 64.8 us; the launch traced here: 64.6 us
  Pallas kernels  61.8 us (95%)
  other arithmetic  1.52 us (2%)
  between operations  0.65 us (1%)
    pallas_call x1, Pallas kernels, local(): pl.pallas_call(functools.partial(kernel, lay, owned * lay.n_dom), out_sha...  61.8 us
    convert_element_type x1, other arithmetic, local(): return (last.astype(BF16), gram)  1.52 us

profile of v5, /device:TPU:1, one launch (start us, length us, event | category | flops | bytes accessed | tf_op | source)
XLA Modules:
  0.0 64.6 jit_solution(9878829965117483289)
XLA Ops:
  0.6 61.8 %shard_map.77 = (f32[8,3072]{1,0:T(8,128)}, f32[8,256]{1,0:T(8,128)}) custom-call(f32[8,3072]{1,0:T(8,128)} %states_hbm.1, s32[16,343]{1,0:T(8,128)} %nodes_hbm.1, f32[16]{0:T(128)} %scale_hbm.1, bf16[343,343]{1,0:T(8,128)(2,1)} %matrix_hbm.1, f32[1,3072]{1,0:T(1,128)} %bitcast.2, f32[1,3072]{1,0:T(1,128)} %bitcast.3), custom_call_target="tpu_custom_call" | custom-call | tf_op jit(solution)/shard_map/pallas_call | solution.py:379
  62.4 0.0 copy-start
  62.5 1.5 %convert_element_type.3 = bf16[8,3072]{1,0:T(8,128)(2,1)} convert(f32[8,3072]{1,0:T(8,128)} %get-tuple-element.4) | non-fusion elementwise | flops 24576 | bytes 147456 | tf_op jit(solution)/shard_map/convert_element_type | solution.py:435
  64.0 0.0 copy-done
  64.0 0.6 copy.9
Async XLA Ops:
  62.4 1.5 %copy-start = (f32[8,256]{1,0:T(8,128)S(1)}, f32[8,256]{1,0:T(8,128)}, u32[]{:S(2)}) copy-start(f32[8,256]{1,0:T(8,128)} %get-tuple-element.9) | copy-start | bytes 24580

commit v6 on v4

--- a/solution.py
+++ b/solution.py
@@ -46,7 +46,7 @@
     filtered, gram, states, nodes, cell_scale, matrix, node_scale, potential,
     lt, lt_half, le, mat, pad_nodes, hb, hb_half, y0, y1, y2, ns, pc, acc, w1, w2, mid, x16, vh,
     stage, init_in, out_low, out_up, in_low, in_up, shares, got, got_edge, part, part_in, sums, sums_in,
-    send_sem, recv_sem, gram_send, gram_recv, load_sem, store_sem,
+    send_sem, recv_sem, gram_send, gram_recv, load_sem, store_sem, known,
 ):
     band, dom = lax.axis_index("band"), lax.axis_index("dom")
     n_band, n_dom = lay.n_band, lay.n_dom
@@ -59,13 +59,33 @@
         lax.rem(my_y + dy, lay.ny) * lay.nz + lax.rem(my_z + dz, lay.nz)
         for dy in (4, 3, 5, 2, 6, 1, 7, 0) for dz in range(lay.nz) if dy or dz
     ]
-    order = [i for i in (n_dom - 1, *range(1, n_dom - 1))]
-    dom_peers = [lax.rem(dom + i, n_dom) for i in order]
+    def around_y(*steps):
+        return [(lax.rem(my_y + i, lay.ny) * lay.nz + my_z, dom) for i in steps]
+
+    def around_z(*steps):
+        return [(my_y * lay.nz + lax.rem(my_z + i, lay.nz), dom) for i in steps if i % lay.nz]
+
+    def around_dom(*steps):
+        return [(band, lax.rem(dom + i, n_dom)) for i in steps if i % n_dom]
+
+    rounds = dict(
+        y1=around_y(1, 7), y2=around_y(2, 6), z1=around_z(1, max(lay.nz - 1, 0)), z2=around_z(2),
+        d1=around_dom(2, 2 * n_dom - 2), d2=around_dom(4, 4 * n_dom - 4), d3=around_dom(8, 8 * n_dom - 8),
+    )
+    slots = {name: i for i, name in enumerate(rounds)}
+
+    def tell(name):
+        for peer in rounds[name]:
+            pl.semaphore_signal(known.at[slots[name]], inc=1, device_id=peer, device_id_type=MESH)
+
+    def hear(name):
+        if rounds[name]:
+            pl.semaphore_wait(known.at[slots[name]], len(rounds[name]))
+
     barrier = pltpu.get_barrier_semaphore()
-    for peer in dom_peers:
-        pl.semaphore_signal(barrier, inc=1, device_id=(band, peer), device_id_type=MESH)
-    for peer in band_peers:
-        pl.semaphore_signal(barrier, inc=1, device_id=(peer, dom), device_id_type=MESH)
+    greeted = [(band, left), (band, right)] + rounds["y1"] + rounds["z1"]
+    for peer in greeted:
+        pl.semaphore_signal(barrier, inc=1, device_id=peer, device_id_type=MESH)
     loads = [
         pltpu.make_async_copy(src, dst, load_sem.at[i])
         for i, (src, dst) in enumerate((
@@ -116,7 +136,7 @@
             [node_scale[:, cols], potential[:, cols], jnp.zeros((6, 384), F32)], axis=0
         )
 
-    pl.semaphore_wait(barrier, len(dom_peers) + len(band_peers))
+    pl.semaphore_wait(barrier, len(greeted))
 
     def rim_copy(src, dst, slot, to):
         copy = pltpu.make_async_remote_copy(
@@ -130,6 +150,7 @@
         rim_copy(stage.at[0], init_in.at[1], 0, left),
         rim_copy(stage.at[1], init_in.at[0], 1, right),
     ]
+    tell("y1")
 
     def gather_mid():
         for p in range(8):
@@ -202,6 +223,7 @@
     gather_mid()
     for copy in started:
         copy.wait_recv()
+    tell("d1")
     for side, tiles in ((0, LOW_TILES[:3]), (1, UP_TILES[3:])):
         there = has_left if side == 0 else has_right
         value = jnp.where(there, init_in[side], 0.0)
@@ -264,6 +286,9 @@
             rim_copy(out_up.at[step, 0:rows], in_low.at[step, 0:rows], 3 + 2 * step, right),
         ]
         started += now
+        if last:
+            hear("z1")
+            tell("z2")
         scatter_mid()
         advance(step, middle, whole)
         if last:
@@ -271,6 +296,7 @@
             advance(step, slice(96, 104), slice(0, 128))
             for share in range(1, 7):
                 fill_share(share)
+            hear("z2")
             for dy in (4, 3, 5, 2, 6, 1, 7, 0):
                 share = lax.rem(my_y + dy, lay.ny)
                 pl.when(jnp.logical_and(share > 0, share < 7))(functools.partial(send_share, share))
@@ -288,6 +314,9 @@
         gather_mid()
         for copy in now:
             copy.wait_recv()
+        for done, following in ((("y1", "y2"), ("d1", "d2")), (("y2", "z1"), ("d2", "d3")))[step]:
+            hear(done)
+            tell(following)
         for i, (lt_, ut_) in enumerate(zip(LOW_TILES, UP_TILES)):
             got_low = jnp.where(has_left, in_low[step, 8 * i : 8 * i + 8], 0.0)
             got_up = jnp.where(has_right, in_up[step, 8 * i : 8 * i + 8], 0.0)
@@ -328,6 +357,7 @@
     columns = got_edge[...].astype(F32).reshape(8 * n_band, 384).astype(BF16)
     sums[...] = (total + dot_t(shares[outer], columns)).astype(BF16)
 
+    hear("d3")
     for i in sorted(range(1, n_dom), key=lambda i: -min(i, n_dom - i)):
         gram_copy(sums, sums_in.at[dom], 3, (band, lax.rem(dom + i, n_dom)))
     sums_in[dom] = sums[...]
@@ -415,6 +445,7 @@
             pltpu.SemaphoreType.DMA((4,)),
             pltpu.SemaphoreType.DMA((6,)),
             pltpu.SemaphoreType.DMA((2,)),
+            pltpu.SemaphoreType.REGULAR((7,)),
         ],
         compiler_params=pltpu.CompilerParams(
             collective_id=0, has_side_effects=True, vmem_limit_bytes=60 * 1024 * 1024

time: 64.2 us -> 64.7 us (level)
  no operation moved by 1% of the time
where the time goes in v6:
time: 64.7 us; the launch traced here: 64.5 us
  Pallas kernels  61.8 us (96%)
  local copies, waits for them, and re-layouts  2.03 us (3%)
  between operations  0.65 us (1%)
    pallas_call x1, Pallas kernels, local(): pl.pallas_call(functools.partial(kernel, lay, owned * lay.n_dom), out_sha...  61.8 us
    unnamed x4, local copies, waits for them, and re-layouts  2.03 us

profile of v6, /device:TPU:1, one launch (start us, length us, event | category | flops | bytes accessed | tf_op | source)
XLA Modules:
  0.0 64.5 jit_solution(10373817631901629323)
XLA Ops:
  0.6 61.8 %shard_map.77 = (bf16[8,3072]{1,0:T(8,128)(2,1)}, f32[8,256]{1,0:T(8,128)}) custom-call(f32[8,3072]{1,0:T(8,128)} %states_hbm.1, s32[16,343]{1,0:T(8,128)} %nodes_hbm.1, f32[16]{0:T(128)} %scale_hbm.1, bf16[343,343]{1,0:T(8,128)(2,1)} %matrix_hbm.1, f32[1,3072]{1,0:T(1,128)} %bitcast.2, f32[1,3072]{1,0:T(1,128)} %bitcast.3), custom_call_target="tpu_custom_call" | custom-call | tf_op jit(solution)/shard_map/pallas_call | solution.py:397
  62.4 0.0 copy-start
  62.4 1.4 %copy.10 = bf16[8,3072]{1,0:T(8,128)(2,1)} copy(bf16[8,3072]{1,0:T(8,128)(2,1)} %get-tuple-element.4) | data formatting | bytes 98304
  63.9 0.0 copy-done
  63.9 0.6 copy.11
Async XLA Ops:
  62.4 1.4 %copy-start = (f32[8,256]{1,0:T(8,128)S(1)}, f32[8,256]{1,0:T(8,128)}, u32[]{:S(2)}) copy-start(f32[8,256]{1,0:T(8,128)} %get-tuple-element.5) | copy-start | bytes 24580
